TPU v7x, 32 devices: a whole 2x2x4 slice. The times are simulated.
32 devices in a mesh: dp: 8 (over y, x, core), tensor: 4 (over z).
Axes of the slice: x: 2, y: 2, z: 4, core: 2. Of those that a mesh axis runs over, the one named last changes fastest.
Arguments:
- tokens: bfloat16 [80, 197, 768], P('dp', None, 'tensor'), may hold values from -6 to 6
- cotangent: bfloat16 [80, 197, 768], P('dp', None, 'tensor'), may hold values from -6 to 6
- live_count: int32 [8], P('dp'), may hold values from 1 to 10, as said below
- ln_scale: bfloat16 [2, 2, 768], P(None, None, 'tensor'), may hold values from 0.099609375 to 1.8984375
- ln_shift: bfloat16 [2, 2, 768], P(None, None, 'tensor'), may hold values from -3 to 3
- w_qkv: bfloat16 [2, 3, 768, 768], P(None, None, None, 'tensor'), may hold values from -0.21875 to 0.21875
- b_qv: bfloat16 [2, 2, 768], P(None, None, 'tensor'), may hold values from -3 to 3
- w_out: bfloat16 [2, 768, 768], P(None, 'tensor'), may hold values from -1.25 to 1.25
- b_out: bfloat16 [2, 768], P(None, 'tensor'), may hold values from -3 to 3
- w_up: bfloat16 [2, 768, 3072], P(None, None, 'tensor'), may hold values from -0.21875 to 0.21875
- b_up: bfloat16 [2, 3072], P(None, 'tensor'), may hold values from -3 to 3
- w_down: bfloat16 [2, 3072, 768], P(None, 'tensor'), may hold values from -0.109375 to 0.109375
- b_down: bfloat16 [2, 768], P(None, 'tensor'), may hold values from -3 to 3
Outputs:
- activations: bfloat16 [80, 197, 768], P('dp', None, 'tensor')
- grad_input: float32 [80, 197, 768], P('dp', None, 'tensor')
- grad_ln_scale: float32 [2, 2, 768], P(None, None, 'tensor')
- grad_ln_shift: float32 [2, 2, 768], P(None, None, 'tensor')
- grad_w_qkv: float32 [2, 3, 768, 768], P(None, None, None, 'tensor')
- grad_b_qv: float32 [2, 2, 768], P(None, None, 'tensor')
- grad_w_out: float32 [2, 768, 768], P(None, 'tensor')
- grad_b_out: float32 [2, 768], P(None, 'tensor')
- grad_w_up: float32 [2, 768, 3072], P(None, None, 'tensor')
- grad_b_up: float32 [2, 3072], P(None, 'tensor')
- grad_w_down: float32 [2, 3072, 768], P(None, 'tensor')
- grad_b_down: float32 [2, 768], P(None, 'tensor')
Inputs may be any that keep to these rules, and one draw needn't show every extreme that they name: Dp index i holds live_count[i] images in its first slots; its other slots of 10 are empty; some index is full and some holds one image.
All inputs are finite; a program needn't handle non-finite values.
Results may differ from a plain program's by a relative error of at most 0.023.
Values may be sent and summed in bfloat16 or wider, within the bound.
A program may use at most 192 MiB of HBM per device.

v0:
```python
import jax
import jax.numpy as jnp
from jax import lax
from jax.sharding import PartitionSpec as P

HEAD = 64
LAYERS = 2


EPSILON = 1e-06


def gelu_exact(values):
    return jax.nn.gelu(values, approximate=False)


def normalize(gathered, gain, shift):
    center = gathered.astype(jnp.float32)
    center = center - jnp.mean(center, -1, keepdims=True)
    factor = lax.rsqrt(jnp.mean(center * center, -1, keepdims=True) + EPSILON)
    unit = center * factor
    return (unit * gain.astype(jnp.float32) + shift.astype(jnp.float32), unit, factor)


def gather_rows(part, gain, shift):
    return (
        lax.all_gather(part, "tensor", axis=1, tiled=True),
        lax.all_gather(gain, "tensor", axis=0, tiled=True),
        lax.all_gather(shift, "tensor", axis=0, tiled=True),
    )


def reduce_rows(term):
    return lax.psum_scatter(
        term.astype(jnp.bfloat16), "tensor", scatter_dimension=1, tiled=True
    ).astype(jnp.float32)


def gather_grad(part):
    return lax.all_gather(part, "tensor", axis=1, tiled=True)


def norm_backward(partial_grad, unit, factor, own_gain, tensor_rank, feat_width):
    full_width = unit.shape[-1]
    own_unit = lax.dynamic_slice_in_dim(unit, tensor_rank * feat_width, feat_width, 1)
    own_grad = lax.psum_scatter(
        partial_grad.astype(jnp.bfloat16), "tensor", scatter_dimension=1, tiled=True
    ).astype(jnp.float32)
    gained = own_grad * own_gain.astype(jnp.float32)
    first_sum, second_sum = lax.psum(
        (jnp.sum(gained, -1), jnp.sum(gained * own_unit, -1)), "tensor"
    )
    first_mean = first_sum[:, None] / full_width
    second_mean = second_sum[:, None] / full_width
    own_back = factor * (gained - first_mean - own_unit * second_mean)
    return (own_back, jnp.sum(own_grad * own_unit, 0), jnp.sum(own_grad, 0))


def on_device(
    tokens,
    cotangent,
    live_count,
    ln_scale,
    ln_shift,
    w_qkv,
    b_qv,
    w_out,
    b_out,
    w_up,
    b_up,
    w_down,
    b_down,
):
    slot_count, length, feat_width = tokens.shape
    row_count = slot_count * length
    tensor_rank = lax.axis_index("tensor")
    local_width = w_qkv.shape[-1]
    head_count = local_width // HEAD
    score_scale = HEAD ** (-0.5)
    live_mask = (jnp.arange(slot_count, dtype=jnp.int32) < live_count[0]).astype(jnp.float32)[
        :, None, None
    ]
    state = tokens.reshape(row_count, feat_width)
    stored = []
    for layer_id in range(LAYERS):
        gathered, gain_one, shift_one = gather_rows(
            state, ln_scale[layer_id, 0], ln_shift[layer_id, 0]
        )
        normed, unit_one, factor_one = normalize(gathered, gain_one, shift_one)
        normed = normed.astype(jnp.bfloat16)
        projected = jnp.einsum(
            "rd,cde->cre", normed, w_qkv[layer_id], preferred_element_type=jnp.float32
        )
        queries = (projected[0] + b_qv[layer_id, 0].astype(jnp.float32)).astype(jnp.bfloat16)
        key_rows = projected[1].astype(jnp.bfloat16)
        values = (projected[2] + b_qv[layer_id, 1].astype(jnp.float32)).astype(jnp.bfloat16)
        queries = queries.reshape(slot_count, length, head_count, HEAD)
        key_rows = key_rows.reshape(slot_count, length, head_count, HEAD)
        values = values.reshape(slot_count, length, head_count, HEAD)
        scores = (
            jnp.einsum("sqhe,skhe->shqk", queries, key_rows, preferred_element_type=jnp.float32)
            * score_scale
        )
        peak = jnp.max(scores, -1, keepdims=True)
        log_total = peak + jnp.log(jnp.sum(jnp.exp(scores - peak), -1, keepdims=True))
        attention = jnp.exp(scores - log_total).astype(jnp.bfloat16)
        mixture = jnp.einsum(
            "shqk,skhe->sqhe", attention, values, preferred_element_type=jnp.float32
        )
        mixture = mixture.astype(jnp.bfloat16).reshape(row_count, local_width)
        attended = reduce_rows(
            jnp.dot(mixture, w_out[layer_id], preferred_element_type=jnp.float32)
        )
        middle = (
            state.astype(jnp.float32) + attended + b_out[layer_id].astype(jnp.float32)
        ).astype(jnp.bfloat16)
        gathered_two, gain_two, shift_two = gather_rows(
            middle, ln_scale[layer_id, 1], ln_shift[layer_id, 1]
        )
        normed_two, unit_two, factor_two = normalize(gathered_two, gain_two, shift_two)
        normed_two = normed_two.astype(jnp.bfloat16)
        hidden = jnp.dot(normed_two, w_up[layer_id], preferred_element_type=jnp.float32) + b_up[
            layer_id
        ].astype(jnp.float32)
        active = gelu_exact(hidden).astype(jnp.bfloat16)
        branch = reduce_rows(jnp.dot(active, w_down[layer_id], preferred_element_type=jnp.float32))
        stored.append(
            (
                unit_one,
                factor_one,
                normed,
                queries,
                key_rows,
                values,
                log_total,
                mixture,
                unit_two,
                factor_two,
                normed_two,
                hidden,
                active,
            )
        )
        state = (middle.astype(jnp.float32) + branch + b_down[layer_id].astype(jnp.float32)).astype(
            jnp.bfloat16
        )
    activations = (
        state.reshape(slot_count, length, feat_width).astype(jnp.float32) * live_mask
    ).astype(jnp.bfloat16)
    upstream = (cotangent.astype(jnp.float32) * live_mask).reshape(row_count, feat_width)
    layer_grads = [None] * LAYERS
    for layer_id in reversed(range(LAYERS)):
        (
            unit_one,
            factor_one,
            normed,
            queries,
            key_rows,
            values,
            log_total,
            mixture,
            unit_two,
            factor_two,
            normed_two,
            hidden,
            active,
        ) = stored[layer_id]
        grad_full = gather_grad(upstream.astype(jnp.bfloat16))
        grad_b_down = jnp.sum(upstream, 0)
        grad_w_down = jnp.einsum("rf,rd->fd", active, grad_full, preferred_element_type=jnp.float32)
        grad_active = jnp.einsum(
            "rd,fd->rf", grad_full, w_down[layer_id], preferred_element_type=jnp.float32
        )
        gelu_pull = jax.vjp(gelu_exact, hidden)[1]
        grad_hidden = gelu_pull(grad_active)[0]
        grad_b_up = jnp.sum(grad_hidden, 0)
        hidden_low = grad_hidden.astype(jnp.bfloat16)
        grad_w_up = jnp.einsum(
            "rd,rf->df", normed_two, hidden_low, preferred_element_type=jnp.float32
        )
        partial_two = jnp.einsum(
            "rf,df->rd", hidden_low, w_up[layer_id], preferred_element_type=jnp.float32
        )
        back_two, scale_two, shift_grad_two = norm_backward(
            partial_two, unit_two, factor_two, ln_scale[layer_id, 1], tensor_rank, feat_width
        )
        grad_middle = upstream + back_two
        grad_b_out = jnp.sum(grad_middle, 0)
        middle_full = gather_grad(grad_middle.astype(jnp.bfloat16))
        grad_w_out = jnp.einsum(
            "re,rd->ed", mixture, middle_full, preferred_element_type=jnp.float32
        )
        grad_mixture = jnp.einsum(
            "rd,ed->re", middle_full, w_out[layer_id], preferred_element_type=jnp.float32
        )
        grad_mixture = grad_mixture.astype(jnp.bfloat16).reshape(
            slot_count, length, head_count, HEAD
        )
        scores = (
            jnp.einsum("sqhe,skhe->shqk", queries, key_rows, preferred_element_type=jnp.float32)
            * score_scale
        )
        attention = jnp.exp(scores - log_total)
        attention_low = attention.astype(jnp.bfloat16)
        grad_attention = jnp.einsum(
            "sqhe,skhe->shqk", grad_mixture, values, preferred_element_type=jnp.float32
        )
        row_delta = jnp.sum(grad_attention * attention, -1, keepdims=True)
        grad_scores = (attention * (grad_attention - row_delta) * score_scale).astype(jnp.bfloat16)
        grad_values = jnp.einsum(
            "shqk,sqhe->skhe", attention_low, grad_mixture, preferred_element_type=jnp.float32
        )
        grad_queries = jnp.einsum(
            "shqk,skhe->sqhe", grad_scores, key_rows, preferred_element_type=jnp.float32
        )
        grad_keys = jnp.einsum(
            "shqk,sqhe->skhe", grad_scores, queries, preferred_element_type=jnp.float32
        )
        grad_stack = jnp.stack([grad_queries, grad_keys, grad_values]).reshape(
            3, row_count, local_width
        )
        grad_b_qv = jnp.stack([jnp.sum(grad_stack[0], 0), jnp.sum(grad_stack[2], 0)])
        stack_low = grad_stack.astype(jnp.bfloat16)
        grad_w_qkv = jnp.einsum(
            "rd,cre->cde", normed, stack_low, preferred_element_type=jnp.float32
        )
        partial_one = jnp.einsum(
            "cre,cde->rd", stack_low, w_qkv[layer_id], preferred_element_type=jnp.float32
        )
        back_one, scale_one, shift_grad_one = norm_backward(
            partial_one, unit_one, factor_one, ln_scale[layer_id, 0], tensor_rank, feat_width
        )
        upstream = grad_middle + back_one
        grad_scale = jnp.stack([scale_one, scale_two])
        grad_shift = jnp.stack([shift_grad_one, shift_grad_two])
        layer_grads[layer_id] = (
            grad_scale,
            grad_shift,
            grad_w_qkv,
            grad_b_qv,
            grad_w_out,
            grad_b_out,
            grad_w_up,
            grad_b_up,
            grad_w_down,
            grad_b_down,
        )
    stacked = tuple((jnp.stack([entry[member] for entry in layer_grads]) for member in range(10)))
    stacked = lax.psum(
        (
            stacked[0],
            stacked[1],
            stacked[2],
            stacked[3],
            stacked[4],
            stacked[5],
            stacked[6],
            stacked[7],
            stacked[8],
            stacked[9],
        ),
        "dp",
    )
    grad_input = upstream.reshape(slot_count, length, feat_width)
    return (
        activations,
        grad_input,
        stacked[0],
        stacked[1],
        stacked[2],
        stacked[3],
        stacked[4],
        stacked[5],
        stacked[6],
        stacked[7],
        stacked[8],
        stacked[9],
    )


def solution(mesh):
    placed = (
        P("dp", None, "tensor"),
        P("dp", None, "tensor"),
        P("dp"),
        P(None, None, "tensor"),
        P(None, None, "tensor"),
        P(None, None, None, "tensor"),
        P(None, None, "tensor"),
        P(None, "tensor", None),
        P(None, "tensor"),
        P(None, None, "tensor"),
        P(None, "tensor"),
        P(None, "tensor", None),
        P(None, "tensor"),
    )
    return jax.shard_map(
        on_device,
        mesh=mesh,
        in_specs=placed,
        out_specs=(
            P("dp", None, "tensor"),
            P("dp", None, "tensor"),
            P(None, None, "tensor"),
            P(None, None, "tensor"),
            P(None, None, None, "tensor"),
            P(None, None, "tensor"),
            P(None, "tensor", None),
            P(None, "tensor"),
            P(None, None, "tensor"),
            P(None, "tensor"),
            P(None, "tensor", None),
            P(None, "tensor"),
        ),
        check_vma=False,
    )
```

profile of v0, /device:TPU:0, one launch (start us, length us, event | category | flops | bytes accessed | tf_op | source)
XLA Modules:
  0.0 1625.9 jit_solution(12858792963363681924)
XLA Ops:
  17.4 21.2 %all-reduce.14 = (bf16[768]{0:T(1024)(128)(2,1)S(1)}, bf16[768]{0:T(1024)(128)(2,1)S(1)}, bf16[768]{0:T(1024)(128)(2,1)S(1)}, bf16[768]{0:T(1024)(128)(2,1)S(1)}...) all-reduce(bf16[768]{0:T(1024)(128)(2,1)S(1)} %dynamic-update-slice, ...), channel_id=9, replica_groups=mesh['dp'=8,'tensor'=4] {'tensor'}, use_global_device_ids=true, to_apply=%add.7 | all-reduce | flops 6144 | bytes 24576
  40.5 37.7 %all-gather.17.cloned.1.call-done = bf16[1970,768]{0,1:T(8,128)(2,1)} async-done(((bf16[1970,192]{0,1:T(8,128)(2,1)}), bf16[1970,768]{0,1:T(8,128)(2,1)}) %all-gather.17.cloned.1.call-update) | async-done | bytes 3025936 | tf_op jit(solution)/shard_map/all_gather | solution.py:27
  89.1 4.0 squeeze.45
  93.2 4.8 convert_element_type.314
  98.0 5.1 squeeze.46
  106.5 3.6 multiply_reduce_fusion.3
  115.7 3.9 convolution_convert_fusion.5
  119.7 59.0 %reduce-scatter.9.cloned.1.call-done = bf16[1970,192]{0,1:T(8,128)(2,1)} async-done(((bf16[1970,768]{0,1:T(8,128)(2,1)}), bf16[1970,192]{0,1:T(8,128)(2,1)}) %reduce-scatter.9.cloned.1.call-update) | async-done | bytes 756496 | tf_op jit(solution)/shard_map/reduce_scatter | solution.py:34
  181.1 63.5 %all-gather.19.cloned.1.call-done = bf16[1970,768]{0,1:T(8,128)(2,1)} async-done(((bf16[1970,192]{0,1:T(8,128)(2,1)}), bf16[1970,768]{0,1:T(8,128)(2,1)}) %all-gather.19.cloned.1.call-update) | async-done | bytes 3025936 | tf_op jit(solution)/shard_map/all_gather | solution.py:27
  250.0 19.4 %multiply_convert_fusion.3 = (bf16[1970,768]{1,0:T(8,128)(2,1)S(1)}, f32[1970,768]{1,0:T(8,128)}, f32[1970,768]{1,0:T(8,128)}) fusion(f32[768]{0:T(1024)S(1)} %get-tuple-element.65, bf16[2,768,768]{2,1,0:T(8,128)(2,1)S(1)} %copy-done.82, f32[768]{0:T(1024)S(1)} %convert_element_type.404, f32[768]{0:T(1024)S(1)} %convert_element_type.403, ...), kind=kOutput, calls=%fused_computation.57 | convolution fusion | flops 2432839680 | bytes 19483648 | tf_op jit(solution)/shard_map/dot_general | solution.py:122
  271.2 4.1 convolution_convert_fusion.3
  275.4 59.0 %reduce-scatter.11.cloned.1.call-done = bf16[1970,192]{0,1:T(8,128)(2,1)} async-done(((bf16[1970,768]{0,1:T(8,128)(2,1)}), bf16[1970,192]{0,1:T(8,128)(2,1)}) %reduce-scatter.11.cloned.1.call-update) | async-done | bytes 756496 | tf_op jit(solution)/shard_map/reduce_scatter | solution.py:34
  336.9 63.4 %all-gather.21.cloned.1.call-done = bf16[1970,768]{0,1:T(8,128)(2,1)} async-done(((bf16[1970,192]{0,1:T(8,128)(2,1)}), bf16[1970,768]{0,1:T(8,128)(2,1)}) %all-gather.21.cloned.1.call-update) | async-done | bytes 3025936 | tf_op jit(solution)/shard_map/all_gather | solution.py:27
  411.2 4.2 squeeze.104
  415.4 4.8 convert_element_type.341
  420.2 4.9 squeeze.105
  428.5 3.6 multiply_reduce_fusion.2
  437.7 3.9 convolution_convert_fusion.4
  441.6 59.0 %reduce-scatter.13.cloned.1.call-done = bf16[1970,192]{0,1:T(8,128)(2,1)} async-done(((bf16[1970,768]{0,1:T(8,128)(2,1)}), bf16[1970,192]{0,1:T(8,128)(2,1)}) %reduce-scatter.13.cloned.1.call-update) | async-done | bytes 756496 | tf_op jit(solution)/shard_map/reduce_scatter | solution.py:34
  503.2 63.4 %all-gather.23.cloned.1.call-done = bf16[1970,768]{0,1:T(8,128)(2,1)} async-done(((bf16[1970,192]{0,1:T(8,128)(2,1)}), bf16[1970,768]{0,1:T(8,128)(2,1)}) %all-gather.23.cloned.1.call-update) | async-done | bytes 3025936 | tf_op jit(solution)/shard_map/all_gather | solution.py:27
  572.0 19.0 %multiply_convert_fusion.2 = (bf16[1970,768]{1,0:T(8,128)(2,1)S(1)}, f32[1970,768]{1,0:T(8,128)}, f32[1970,768]{1,0:T(8,128)}) fusion(f32[768]{0:T(1024)S(1)} %get-tuple-element.64, bf16[2,768,768]{2,1,0:T(8,128)(2,1)S(1)} %copy-done.83, f32[768]{0:T(1024)S(1)} %convert_element_type.408, f32[768]{0:T(1024)S(1)} %convert_element_type.407, ...), kind=kOutput, calls=%fused_computation.44 | convolution fusion | flops 2432839680 | bytes 19483648 | tf_op jit(solution)/shard_map/dot_general | solution.py:122
  592.6 4.1 convolution_convert_fusion.2
  600.1 55.6 %reduce-scatter.15.cloned.1.call-done = bf16[1970,192]{0,1:T(8,128)(2,1)} async-done(((bf16[1970,768]{0,1:T(8,128)(2,1)}), bf16[1970,192]{0,1:T(8,128)(2,1)}) %reduce-scatter.15.cloned.1.call-update) | async-done | bytes 756496 | tf_op jit(solution)/shard_map/reduce_scatter | solution.py:34
  664.2 4.6 fusion.199
  676.6 63.6 %all-gather.25.cloned.1.call-done = bf16[1970,768]{0,1:T(8,128)(2,1)} async-done(((bf16[1970,192]{0,1:T(8,128)(2,1)}), bf16[1970,768]{0,1:T(8,128)(2,1)}) %all-gather.25.cloned.1.call-update) | async-done | bytes 3025936 | tf_op jit(solution)/shard_map/all_gather | solution.py:40
  740.2 10.9 fusion.219
  752.8 4.0 convolution_convert_fusion.1
  756.8 3.6 fusion.8
  762.8 53.0 %reduce-scatter.17.cloned.1.call-done = bf16[1970,192]{0,1:T(8,128)(2,1)} async-done(((bf16[1970,768]{0,1:T(8,128)(2,1)}), bf16[1970,192]{0,1:T(8,128)(2,1)}) %reduce-scatter.17.cloned.1.call-update) | async-done | bytes 756496 | tf_op jit(solution)/shard_map/reduce_scatter | solution.py:46
  818.7 17.5 %all-reduce.13 = (f32[1970]{0:T(1024)S(1)}, f32[1970]{0:T(1024)S(1)}) all-reduce(f32[1970]{0:T(1024)S(1)} %get-tuple-element.55, f32[1970]{0:T(1024)S(1)} %get-tuple-element.56), channel_id=1, replica_groups=mesh['dp'=8,'tensor'=4] {'tensor'}, use_global_device_ids=true, to_apply=%region_20.0 | all-reduce | flops 3940 | bytes 31520 | tf_op jit(solution)/shard_map/psum | solution.py:50
  841.2 62.0 %all-gather.27.cloned.1.call-done = bf16[1970,768]{0,1:T(8,128)(2,1)} async-done(((bf16[1970,192]{0,1:T(8,128)(2,1)}), bf16[1970,768]{0,1:T(8,128)(2,1)}) %all-gather.27.cloned.1.call-update) | async-done | bytes 3025936 | tf_op jit(solution)/shard_map/all_gather | solution.py:40
  906.7 4.3 reshape.267
  911.1 4.4 fusion.155
  915.5 13.5 bitcast_convert_fusion.5
  929.0 12.2 fusion.119
  941.2 5.6 bitcast_convert_fusion.4
  958.1 6.3 bitcast_convert_fusion.1
  964.5 3.6 fusion.6
  968.1 55.4 %reduce-scatter.19.cloned.1.call-done = bf16[1970,192]{0,1:T(8,128)(2,1)} async-done(((bf16[1970,768]{0,1:T(8,128)(2,1)}), bf16[1970,192]{0,1:T(8,128)(2,1)}) %reduce-scatter.19.cloned.1.call-update) | async-done | bytes 756496 | tf_op jit(solution)/shard_map/reduce_scatter | solution.py:46
  1026.4 17.5 %all-reduce.12 = (f32[1970]{0:T(1024)S(1)}, f32[1970]{0:T(1024)S(1)}) all-reduce(f32[1970]{0:T(1024)S(1)} %get-tuple-element.53, f32[1970]{0:T(1024)S(1)} %get-tuple-element.57), channel_id=1, replica_groups=mesh['dp'=8,'tensor'=4] {'tensor'}, use_global_device_ids=true, to_apply=%region_26.0 | all-reduce | flops 3940 | bytes 31520 | tf_op jit(solution)/shard_map/psum | solution.py:50
  1049.3 62.0 %all-gather.29.cloned.1.call-done = bf16[1970,768]{0,1:T(8,128)(2,1)} async-done(((bf16[1970,192]{0,1:T(8,128)(2,1)}), bf16[1970,768]{0,1:T(8,128)(2,1)}) %all-gather.29.cloned.1.call-update) | async-done | bytes 3025936 | tf_op jit(solution)/shard_map/all_gather | solution.py:40
  1111.3 10.2 fusion.220
  1123.2 4.0 convolution_convert_fusion
  1127.3 3.6 fusion.4
  1130.9 55.4 %reduce-scatter.21.cloned.1.call-done = bf16[1970,192]{0,1:T(8,128)(2,1)} async-done(((bf16[1970,768]{0,1:T(8,128)(2,1)}), bf16[1970,192]{0,1:T(8,128)(2,1)}) %reduce-scatter.21.cloned.1.call-update) | async-done | bytes 756496 | tf_op jit(solution)/shard_map/reduce_scatter | solution.py:46
  1189.2 17.5 %all-reduce.11 = (f32[1970]{0:T(1024)S(1)}, f32[1970]{0:T(1024)S(1)}) all-reduce(f32[1970]{0:T(1024)S(1)} %get-tuple-element.51, f32[1970]{0:T(1024)S(1)} %get-tuple-element.58), channel_id=1, replica_groups=mesh['dp'=8,'tensor'=4] {'tensor'}, use_global_device_ids=true, to_apply=%region_31.0 | all-reduce | flops 3940 | bytes 31520 | tf_op jit(solution)/shard_map/psum | solution.py:50
  1212.2 62.0 %all-gather.31.cloned.1.call-done = bf16[1970,768]{0,1:T(8,128)(2,1)} async-done(((bf16[1970,192]{0,1:T(8,128)(2,1)}), bf16[1970,768]{0,1:T(8,128)(2,1)}) %all-gather.31.cloned.1.call-update) | async-done | bytes 3025936 | tf_op jit(solution)/shard_map/all_gather | solution.py:40
  1274.2 3.6 convolution_convert_fusion.6
  1277.8 5.0 reshape.268
  1282.8 6.3 fusion.151
  1289.0 13.3 bitcast_convert_fusion.3
  1302.4 12.6 fusion.116
  1315.0 6.3 bitcast_convert_fusion.2
  1323.1 4.0 stack.172
  1332.2 3.7 stack.173
  1338.8 3.7 stack.174
  1346.6 6.2 bitcast_convert_fusion
  1353.0 5.6 convolution_bitcast_fusion
  1386.3 3.6 fusion.2
  1414.2 17.5 %all-reduce.10 = (f32[1970]{0:T(1024)S(1)}, f32[1970]{0:T(1024)S(1)}) all-reduce(f32[1970]{0:T(1024)S(1)} %get-tuple-element.49, f32[1970]{0:T(1024)S(1)} %get-tuple-element.59), channel_id=1, replica_groups=mesh['dp'=8,'tensor'=4] {'tensor'}, use_global_device_ids=true, to_apply=%region_37.0 | all-reduce | flops 3940 | bytes 31520 | tf_op jit(solution)/shard_map/psum | solution.py:50
  1435.0 4.0 reshape.365
  1441.5 24.4 %all-reduce.8 = (f32[2,2,192]{2,1,0:T(2,128)}, f32[2,2,192]{2,1,0:T(2,128)}, f32[2,2,192]{2,1,0:T(2,128)}, f32[2,192]{1,0:T(2,128)}, f32[2,768]{1,0:T(2,128)}, /*index=5*/f32[2,192]{1,0:T(2,128)}) all-reduce(f32[2,2,192]{2,1,0:T(2,128)S(1)} %pad_maximum_fusion.5, ...), channel_id=1, replica_groups=mesh['dp'=8,'tensor'=4] {'dp'}, use_global_device_ids=true, to_apply=%region_42.0 | all-reduce | flops 4608 | bytes 36864 | tf_op jit(solution)/shard_map/psum | solution.py:249
  1465.9 142.2 %all-reduce.17.cloned.1.call-done = (f32[2,3,768,192]{2,3,1,0:T(8,128)}, f32[2,192,768]{2,1,0:T(8,128)}, f32[2,768,768]{2,1,0:T(8,128)}, f32[2,768,768]{2,1,0:T(8,128)}) async-done(((f32[2,3,768,192]{2,3,1,0:T(8,128)}, f32[2,192,768]{2,1,0:T(8,128)}, f32[2,768,768]{2,1,0:T(8,128)}, f32[2,768,768]{2,1,0:T(8,128)}), (f32[2,3,768,192]{2,3,1,0:T(8,128)}, f32[2,192,768]{2,1,0:T(8,128)}, ...) | async-done | bytes 14155792 | tf_op jit(solution)/shard_map/psum | solution.py:249
  1608.1 4.3 copy.227
  (389 shorter events, 214.7 us)
Async XLA Ops:
  7.2 32.3 %copy-start.31 = (bf16[2,3,768,192]{2,3,1,0:T(8,128)(2,1)S(1)}, bf16[2,3,768,192]{2,3,1,0:T(8,128)(2,1)}, u32[]{:S(2)}) copy-start(bf16[2,3,768,192]{2,3,1,0:T(8,128)(2,1)} %param.18) | copy-start | bytes 5308420
  7.2 71.1 %all-gather.17.cloned.1.call-start = ((), (), s32[]{:S(2)}) async-start(), calls=%async_computation.8 | async-start | bytes 3932160 | tf_op jit(solution)/shard_map/all_gather | solution.py:27
  11.6 167.1 %reduce-scatter.9.cloned.1.call-start = ((), (), s32[]{:S(2)}) async-start(), calls=%async_computation.9 | async-start | bytes 3932160 | tf_op jit(solution)/shard_map/reduce_scatter | solution.py:34
  38.6 47.6 %copy-start.64 = (f32[768]{0:T(1024)}, f32[768]{0:T(1024)S(1)}, u32[]{:S(2)}) copy-start(f32[768]{0:T(1024)S(1)} %convert_element_type.402) | copy-start | bytes 9220
  38.6 47.6 %copy-start.66 = (f32[768]{0:T(1024)}, f32[768]{0:T(1024)S(1)}, u32[]{:S(2)}) copy-start(f32[768]{0:T(1024)S(1)} %convert_element_type.401) | copy-start | bytes 9220
  113.9 64.7 %copy-start.23 = (bf16[1970,192]{0,1:T(8,128)(2,1)S(1)}, bf16[1970,192]{0,1:T(8,128)(2,1)}, u32[]{:S(2)}) copy-start(bf16[1970,192]{0,1:T(8,128)(2,1)} %reshape.366) | copy-start | bytes 2269444
  115.6 65.3 %copy-start.15 = (bf16[1970,192]{0,1:T(8,128)(2,1)}, bf16[1970,192]{0,1:T(8,128)(2,1)S(1)}, u32[]{:S(2)}) copy-start(bf16[1970,192]{0,1:T(8,128)(2,1)S(1)} %reshape.264) | copy-start | bytes 2269444
  115.7 65.4 %copy-start.52 = (bf16[2,768]{1,0:T(2,128)(2,1)S(1)}, bf16[2,768]{1,0:T(2,128)(2,1)}, u32[]{:S(2)}) copy-start(bf16[2,768]{1,0:T(2,128)(2,1)} %param.23) | copy-start | bytes 9220
  119.6 125.0 %all-gather.19.cloned.1.call-start = ((), (), s32[]{:S(2)}) async-start(), calls=%async_computation.10 | async-start | bytes 3932160 | tf_op jit(solution)/shard_map/all_gather | solution.py:27
  180.9 153.4 %reduce-scatter.11.cloned.1.call-start = ((), (), s32[]{:S(2)}) async-start(), calls=%async_computation.11 | async-start | bytes 3932160 | tf_op jit(solution)/shard_map/reduce_scatter | solution.py:34
  181.0 88.4 %copy-start.68 = (f32[768]{0:T(1024)}, f32[768]{0:T(1024)S(1)}, u32[]{:S(2)}) copy-start(f32[768]{0:T(1024)S(1)} %convert_element_type.404) | copy-start | bytes 9220
  181.0 88.4 %copy-start.70 = (f32[768]{0:T(1024)}, f32[768]{0:T(1024)S(1)}, u32[]{:S(2)}) copy-start(f32[768]{0:T(1024)S(1)} %convert_element_type.403) | copy-start | bytes 9220
  181.1 88.4 %copy-start.62 = (f32[768]{0:T(1024)}, f32[768]{0:T(1024)S(1)}, u32[]{:S(2)}) copy-start(f32[768]{0:T(1024)S(1)} %get-tuple-element.65) | copy-start | bytes 9220
  181.1 68.9 %copy-start.82 = (bf16[2,768,768]{2,1,0:T(8,128)(2,1)S(1)}, bf16[2,768,768]{2,1,0:T(8,128)(2,1)}, u32[]{:S(2)}) copy-start(bf16[2,768,768]{2,1,0:T(8,128)(2,1)} %param.22) | copy-start | bytes 7077892
  247.2 22.2 %copy-start.44 = (f32[1970]{0:T(1024)}, f32[1970]{0:T(1024)S(1)}, u32[]{:S(2)}) copy-start(f32[1970]{0:T(1024)S(1)} %broadcast_multiply_fusion.10) | copy-start | bytes 23644
  250.0 19.5 %copy-start.46 = (f32[1970]{0:T(1024)}, f32[1970]{0:T(1024)S(1)}, u32[]{:S(2)}) copy-start(f32[1970]{0:T(1024)S(1)} %add_rsqrt_fusion.2) | copy-start | bytes 23644
  250.0 21.1 %copy-start.79 = (bf16[2,768,768]{2,1,0:T(8,128)(2,1)S(1)}, bf16[2,768,768]{2,1,0:T(8,128)(2,1)}, u32[]{:S(2)}) copy-start(bf16[2,768,768]{2,1,0:T(8,128)(2,1)} %param.24) | copy-start | bytes 7077892
  271.2 63.2 %copy-start.25 = (bf16[1970,192]{0,1:T(8,128)(2,1)S(1)}, bf16[1970,192]{0,1:T(8,128)(2,1)}, u32[]{:S(2)}) copy-start(bf16[1970,192]{0,1:T(8,128)(2,1)} %add_convert_fusion.11) | copy-start | bytes 2269444
  275.3 130.4 %copy-start.35 = (bf16[1,3,768,192]{2,3,1,0:T(8,128)(2,1)S(1)}, bf16[1,3,768,192]{2,3,1,0:T(8,128)(2,1)}, u32[]{:S(2)}) copy-start(bf16[1,3,768,192]{2,3,1,0:T(8,128)(2,1)} %get-tuple-element.119) | copy-start | bytes 2654212
  275.3 125.0 %all-gather.21.cloned.1.call-start = ((), (), s32[]{:S(2)}) async-start(), calls=%async_computation.12 | async-start | bytes 3932160 | tf_op jit(solution)/shard_map/all_gather | solution.py:27
  336.6 164.0 %reduce-scatter.13.cloned.1.call-start = ((), (), s32[]{:S(2)}) async-start(), calls=%async_computation.13 | async-start | bytes 3932160 | tf_op jit(solution)/shard_map/reduce_scatter | solution.py:34
  336.7 71.5 %copy-start.72 = (f32[768]{0:T(1024)}, f32[768]{0:T(1024)S(1)}, u32[]{:S(2)}) copy-start(f32[768]{0:T(1024)S(1)} %convert_element_type.406) | copy-start | bytes 9220
  336.7 71.5 %copy-start.74 = (f32[768]{0:T(1024)}, f32[768]{0:T(1024)S(1)}, u32[]{:S(2)}) copy-start(f32[768]{0:T(1024)S(1)} %convert_element_type.405) | copy-start | bytes 9220
  436.0 64.7 %copy-start.24 = (bf16[1970,192]{0,1:T(8,128)(2,1)S(1)}, bf16[1970,192]{0,1:T(8,128)(2,1)}, u32[]{:S(2)}) copy-start(bf16[1970,192]{0,1:T(8,128)(2,1)} %add_convert_fusion.10) | copy-start | bytes 2269444
  437.7 65.2 %copy-start.17 = (bf16[1970,192]{0,1:T(8,128)(2,1)}, bf16[1970,192]{0,1:T(8,128)(2,1)S(1)}, u32[]{:S(2)}) copy-start(bf16[1970,192]{0,1:T(8,128)(2,1)S(1)} %reshape.265) | copy-start | bytes 2269444
  441.6 125.0 %all-gather.23.cloned.1.call-start = ((), (), s32[]{:S(2)}) async-start(), calls=%async_computation.14 | async-start | bytes 3932160 | tf_op jit(solution)/shard_map/all_gather | solution.py:27
  502.9 152.8 %reduce-scatter.15.cloned.1.call-start = ((), (), s32[]{:S(2)}) async-start(), calls=%async_computation.15 | async-start | bytes 3932160 | tf_op jit(solution)/shard_map/reduce_scatter | solution.py:34
  572.0 20.6 %copy-start.80 = (bf16[2,768,768]{2,1,0:T(8,128)(2,1)S(1)}, bf16[2,768,768]{2,1,0:T(8,128)(2,1)}, u32[]{:S(2)}) copy-start(bf16[2,768,768]{2,1,0:T(8,128)(2,1)} %param.24) | copy-start | bytes 7077892
  596.7 143.5 %all-gather.25.cloned.1.call-start = ((), (), s32[]{:S(2)}) async-start(), calls=%async_computation.16 | async-start | bytes 3932160 | tf_op jit(solution)/shard_map/all_gather | solution.py:40
  676.5 139.3 %reduce-scatter.17.cloned.1.call-start = ((), (), s32[]{:S(2)}) async-start(), calls=%async_computation.17 | async-start | bytes 3932160 | tf_op jit(solution)/shard_map/reduce_scatter | solution.py:46
  740.2 12.6 copy-start.84
  756.8 146.4 %all-gather.27.cloned.1.call-start = ((), (), s32[]{:S(2)}) async-start(), calls=%async_computation.18 | async-start | bytes 3932160 | tf_op jit(solution)/shard_map/all_gather | solution.py:40
  756.8 59.0 %copy-start.55 = (f32[1,1,192]{2,1,0:T(1,128)S(1)}, f32[1,1,192]{2,1,0:T(1,128)}, u32[]{:S(2)}) copy-start(f32[1,1,192]{2,1,0:T(1,128)} %get-tuple-element.125) | copy-start | bytes 2308
  839.0 72.1 %copy-start.21 = (bf16[10,197,3,64]{1,0,3,2:T(8,128)(2,1)S(1)}, bf16[10,197,3,64]{1,0,3,2:T(8,128)(2,1)}, u32[]{:S(2)}) copy-start(bf16[10,197,3,64]{1,0,3,2:T(8,128)(2,1)} %copy-done.20) | copy-start | bytes 2269444
  841.1 182.4 %reduce-scatter.19.cloned.1.call-start = ((), (), s32[]{:S(2)}) async-start(), calls=%async_computation.19 | async-start | bytes 3932160 | tf_op jit(solution)/shard_map/reduce_scatter | solution.py:46
  915.5 13.5 copy-start.28
  958.1 6.4 copy-start.7
  958.1 6.4 copy-start.49
  958.1 6.4 copy-start.51
  964.4 59.1 %copy-start.54 = (f32[1,1,192]{2,1,0:T(1,128)S(1)}, f32[1,1,192]{2,1,0:T(1,128)}, u32[]{:S(2)}) copy-start(f32[1,1,192]{2,1,0:T(1,128)} %get-tuple-element.124) | copy-start | bytes 2308
  964.5 146.9 %all-gather.29.cloned.1.call-start = ((), (), s32[]{:S(2)}) async-start(), calls=%async_computation.20 | async-start | bytes 3932160 | tf_op jit(solution)/shard_map/all_gather | solution.py:40
  968.1 143.2 %copy-start.63 = (f32[768]{0:T(1024)S(1)}, f32[768]{0:T(1024)}, u32[]{:S(2)}) copy-start(f32[768]{0:T(1024)} %copy-done.62) | copy-start | bytes 9220
  968.1 143.2 %copy-start.81 = (bf16[2,768,768]{2,1,0:T(8,128)(2,1)S(1)}, bf16[2,768,768]{2,1,0:T(8,128)(2,1)}, u32[]{:S(2)}) copy-start(bf16[2,768,768]{2,1,0:T(8,128)(2,1)} %param.24) | copy-start | bytes 7077892
  1049.3 137.0 %reduce-scatter.21.cloned.1.call-start = ((), (), s32[]{:S(2)}) async-start(), calls=%async_computation.21 | async-start | bytes 3932160 | tf_op jit(solution)/shard_map/reduce_scatter | solution.py:46
  1111.3 11.8 copy-start.85
  1127.2 59.1 %copy-start.53 = (f32[1,1,192]{2,1,0:T(1,128)S(1)}, f32[1,1,192]{2,1,0:T(1,128)}, u32[]{:S(2)}) copy-start(f32[1,1,192]{2,1,0:T(1,128)} %get-tuple-element.123) | copy-start | bytes 2308
  1127.2 147.0 %all-gather.31.cloned.1.call-start = ((), (), s32[]{:S(2)}) async-start(), calls=%async_computation.22 | async-start | bytes 3932160 | tf_op jit(solution)/shard_map/all_gather | solution.py:40
  1212.2 199.8 %reduce-scatter.23.cloned.1.call-start = ((), (), s32[]{:S(2)}) async-start(), calls=%async_computation.23 | async-start | bytes 3932160 | tf_op jit(solution)/shard_map/reduce_scatter | solution.py:46
  1277.8 11.3 copy-start.37
  1315.0 6.3 copy-start.34
  1352.9 255.2 %all-reduce.17.cloned.1.call-start = ((), (), s32[]{:S(2)}) async-start(), calls=%async_computation.24 | async-start | bytes 28311552 | tf_op jit(solution)/shard_map/psum | solution.py:249
  1375.9 6.1 copy-start.3
  1375.9 6.1 copy-start.39
  1375.9 6.1 copy-start.41
  1375.9 6.1 copy-start.43
  1375.9 6.1 copy-start.65
  1389.9 15.5 copy-start.22
  1389.9 41.8 %copy-start.12 = (f32[1970,192]{0,1:T(8,128)S(1)}, f32[1970,192]{0,1:T(8,128)}, u32[]{:S(2)}) copy-start(f32[1970,192]{0,1:T(8,128)} %copy-done.11) | copy-start | bytes 4538884
  1434.9 6.5 copy-start.61
  1434.9 6.5 copy-start.60
  1434.9 6.5 copy-start.56
  1434.9 6.6 copy-start.57
  1434.9 6.6 copy-start.58
  1434.9 6.6 copy-start.59
  (50 other events, 180.0 us)
Sparse Core Ops, SparseCore 0:
  11.7 66.4 all-gather.16
  119.7 58.8 reduce-scatter.8
  181.1 63.5 all-gather.18
  275.4 58.8 reduce-scatter.10
  336.8 63.5 all-gather.20
  441.7 58.8 reduce-scatter.12
  503.1 63.5 all-gather.22
  596.8 58.8 reduce-scatter.14
  676.7 63.5 all-gather.24
  756.9 58.8 reduce-scatter.16
  841.2 61.8 all-gather.26
  964.6 58.8 reduce-scatter.18
  1049.4 61.8 all-gather.28
  1127.3 58.8 reduce-scatter.20
  1212.3 61.8 all-gather.30
  1353.0 58.8 reduce-scatter.22
  1417.0 191.0 all-reduce.16
where the time goes:
time: 1640 us; the launch traced here: 1630 us
  waiting for transfers between devices  1020 us (62%)
  matrix products  214 us (13%)
  local copies, waits for them, and re-layouts  148 us (9%)
  blocking collectives  115 us (7%)
  other arithmetic  111 us (7%)
  between operations  16.8 us (1%)
    all_gather x4, waiting for transfers between devices, gather_grad(): return lax.all_gather(part, 'tensor', axis=1, tiled=True)  250 us
    reduce_scatter x4, waiting for transfers between devices, reduce_rows(): lax.psum_scatter(term.astype(jnp.bfloat16), 'tensor', scatter_dimension=1...  233 us
    all_gather x4, waiting for transfers between devices, gather_rows(): lax.all_gather(part, 'tensor', axis=1, tiled=True)  228 us
    reduce_scatter x4, waiting for transfers between devices, norm_backward(): lax.psum_scatter(partial_grad.astype(jnp.bfloat16), 'tensor', scatter_dim...  166 us
    psum x1, waiting for transfers between devices, on_device(): lax.psum((stacked[0], stacked[1], stacked[2], stacked[3], stacked[4], sta...  142 us
    psum x4, blocking collectives, norm_backward(): lax.psum((jnp.sum(gained, -1), jnp.sum(gained * own_unit, -1)), 'tensor')  69.9 us
    unnamed x222, local copies, waits for them, and re-layouts  42.9 us
    dot_general x2, matrix products, on_device(): jnp.dot(normed_two, w_up[layer_id], preferred_element_type=jnp.float32)  38.4 us
  transfers between devices with their start and end apart: 17, of which 17 were waited for; matrix products, arithmetic and copies ran while one was open for 5% of the time, Pallas kernels for 0%

commit v1 on v0

v1 whole, which is shorter than its diff:
```python
import functools

import jax
import jax.numpy as jnp
from jax import lax
from jax.experimental import pallas as pl
from jax.experimental.pallas import tpu as pltpu
from jax.sharding import PartitionSpec as P

HEAD = 64
LAYERS = 2
EPSILON = 1e-06
ALL = ("tensor", "dp")
F32 = jnp.float32
BF16 = jnp.bfloat16
NN = (((1,), (0,)), ((), ()))
NT = (((1,), (1,)), ((), ()))
TN = (((0,), (0,)), ((), ()))


def mul(left, right, form):
    return lax.dot_general(left, right, form, preferred_element_type=F32)


def softmax_columns(keys, queries, length):
    scores = mul(keys, queries, NT) * HEAD ** (-0.5)
    row = lax.broadcasted_iota(jnp.int32, scores.shape, 0)
    scores = jnp.where(row < length, scores, -jnp.inf)
    raised = jnp.exp(scores - jnp.max(scores, 0, keepdims=True))
    return raised * (1.0 / jnp.sum(raised, 0, keepdims=True))


def attention_forward_kernel(qkv_ref, out_ref, *, length):
    width = out_ref.shape[1]
    for head in range(width // HEAD):
        at = head * HEAD
        q = qkv_ref[:, at : at + HEAD]
        k = qkv_ref[:, width + at : width + at + HEAD]
        v = qkv_ref[:, 2 * width + at : 2 * width + at + HEAD]
        probs = softmax_columns(k, q, length)
        out_ref[:, at : at + HEAD] = mul(probs.astype(BF16), v, TN).astype(BF16)


def attention_backward_kernel(qkv_ref, grad_ref, out_ref, *, length):
    width = grad_ref.shape[1]
    for head in range(width // HEAD):
        at = head * HEAD
        q = qkv_ref[:, at : at + HEAD]
        k = qkv_ref[:, width + at : width + at + HEAD]
        v = qkv_ref[:, 2 * width + at : 2 * width + at + HEAD]
        dm = grad_ref[:, at : at + HEAD]
        probs = softmax_columns(k, q, length)
        dp = mul(v, dm, NT)
        delta = jnp.sum(dp * probs, 0, keepdims=True)
        ds = (probs * (dp - delta) * HEAD ** (-0.5)).astype(BF16)
        out_ref[:, at : at + HEAD] = mul(ds, k, TN).astype(BF16)
        out_ref[:, width + at : width + at + HEAD] = mul(ds, q, NN).astype(BF16)
        out_ref[:, 2 * width + at : 2 * width + at + HEAD] = mul(
            probs.astype(BF16), dm, NN
        ).astype(BF16)


def attention_call(kernel, out_width, seq, length, *arrays):
    rows = arrays[0].shape[0]
    heads = arrays[0].shape[1] // (3 * HEAD)
    return pl.pallas_call(
        functools.partial(kernel, length=length),
        grid=(rows // seq,),
        in_specs=[pl.BlockSpec((seq, a.shape[1]), lambda b: (b, 0)) for a in arrays],
        out_specs=pl.BlockSpec((seq, out_width), lambda b: (b, 0)),
        out_shape=jax.ShapeDtypeStruct((rows, out_width), BF16),
        compiler_params=pltpu.CompilerParams(vmem_limit_bytes=32 * 2**20),
        cost_estimate=pl.CostEstimate(
            flops=rows * heads * seq * HEAD * 2 * (2 if len(arrays) == 1 else 5),
            bytes_accessed=rows * 2 * (out_width + sum(a.shape[1] for a in arrays)),
            transcendentals=rows * heads * seq,
        ),
    )(*arrays)


def normalize(values, gain, shift):
    center = values.astype(F32)
    center = center - jnp.mean(center, -1, keepdims=True)
    factor = lax.rsqrt(jnp.mean(center * center, -1, keepdims=True) + EPSILON)
    return (center * factor * gain + shift).astype(BF16)


def normalize_backward(values, gain, grad):
    center = values.astype(F32)
    center = center - jnp.mean(center, -1, keepdims=True)
    factor = lax.rsqrt(jnp.mean(center * center, -1, keepdims=True) + EPSILON)
    unit = center * factor
    gained = grad * gain
    back = factor * (
        gained
        - jnp.mean(gained, -1, keepdims=True)
        - unit * jnp.mean(gained * unit, -1, keepdims=True)
    )
    return back, jnp.sum(grad * unit, 0), jnp.sum(grad, 0)


def own_slice(matrix, rank, parts):
    size = matrix.shape[-1] // parts
    piece = lax.dynamic_slice_in_dim(matrix, rank * size, size, matrix.ndim - 1)
    return jnp.swapaxes(piece, -1, -2)


def own_rows(matrix, rank, parts):
    size = matrix.shape[-2] // parts
    return lax.dynamic_slice_in_dim(matrix, rank * size, size, matrix.ndim - 2)


def gather_all(part):
    return lax.all_gather(part, ALL, axis=0, tiled=False)


def on_device(
    tokens,
    cotangent,
    live_count,
    ln_scale,
    ln_shift,
    w_qkv,
    b_qv,
    w_out,
    b_out,
    w_up,
    b_up,
    w_down,
    b_down,
):
    slot_count, length, feat_width = tokens.shape
    n_dp = lax.axis_size("dp")
    n_tensor = lax.axis_size("tensor")
    devices = n_dp * n_tensor
    dp_rank = lax.axis_index("dp")
    tensor_rank = lax.axis_index("tensor")
    width = feat_width * n_tensor
    ff_width = w_up.shape[-1]
    each = -(-slot_count // n_tensor)
    seq = -(-length // 16) * 16
    rows = each * seq
    live_mask = (jnp.arange(slot_count, dtype=jnp.int32) < live_count[0])[:, None, None]

    def to_images(array):
        array = jnp.pad(array, ((0, each * n_tensor - slot_count), (0, 0), (0, 0)))
        array = array.reshape(n_tensor, each, length, feat_width)
        array = lax.all_to_all(array, "tensor", 0, 0)
        array = array.transpose(1, 2, 0, 3).reshape(each, length, width)
        return jnp.pad(array, ((0, 0), (0, seq - length), (0, 0))).reshape(rows, width)

    def to_slots(array):
        array = array.astype(BF16).reshape(each, seq, n_tensor, feat_width)[:, :length]
        array = lax.all_to_all(array.transpose(2, 0, 1, 3), "tensor", 0, 0)
        return array.reshape(each * n_tensor, length, feat_width)[:slot_count]

    small = [ln_scale, ln_shift, b_qv, b_out, b_up, b_down]
    flat = jnp.concatenate([a.reshape(-1) for a in small])
    flat = lax.all_gather(flat, "tensor", axis=0, tiled=False).astype(F32)
    full, start = [], 0
    for a in small:
        piece = flat[:, start : start + a.size].reshape((n_tensor,) + a.shape)
        start += a.size
        full.append(jnp.moveaxis(piece, 0, -2).reshape(a.shape[:-1] + (n_tensor * a.shape[-1],)))
    scale_f, shift_f, bqv_f, bout_f, bup_f, bdown_f = full

    head_rows = feat_width // n_dp
    up_rows = ff_width // n_dp
    weights = []
    for layer in range(LAYERS):
        one = jnp.concatenate(
            [
                own_slice(w_qkv[layer], dp_rank, n_dp).reshape(3 * head_rows, width),
                own_rows(w_out[layer], dp_rank, n_dp),
            ]
        )
        two = jnp.concatenate(
            [own_slice(w_up[layer], dp_rank, n_dp), own_rows(w_down[layer], dp_rank, n_dp)]
        )
        one = gather_all(one)
        two = gather_all(two)
        qkv_t = (
            one[:, : 3 * head_rows]
            .reshape(devices, 3, head_rows, width)
            .transpose(1, 0, 2, 3)
            .reshape(3 * width, width)
        )
        weights.append(
            (
                qkv_t,
                one[:, 3 * head_rows :].reshape(width, width),
                two[:, :up_rows].reshape(devices * up_rows, width),
                two[:, up_rows:].reshape(devices * up_rows, width),
            )
        )

    state = to_images(tokens)
    grad = to_images(jnp.where(live_mask, cotangent, jnp.zeros_like(cotangent)))
    stored = []
    for layer in range(LAYERS):
        qkv_t, out_w, up_t, down_w = weights[layer]
        normed = normalize(state, scale_f[layer, 0], shift_f[layer, 0])
        bias = jnp.concatenate([bqv_f[layer, 0], jnp.zeros((width,), F32), bqv_f[layer, 1]])
        qkv = (mul(normed, qkv_t, NT) + bias).astype(BF16)
        mixed = attention_call(attention_forward_kernel, width, seq, length, qkv)
        middle = (state.astype(F32) + mul(mixed, out_w, NN) + bout_f[layer]).astype(BF16)
        normed_two = normalize(middle, scale_f[layer, 1], shift_f[layer, 1])
        hidden = mul(normed_two, up_t, NT) + bup_f[layer]
        below = 0.5 + 0.5 * lax.erf(hidden * 0.5**0.5)
        active = (hidden * below).astype(BF16)
        slope = (below + hidden * jnp.exp(-0.5 * hidden * hidden) * 0.3989422804014327).astype(BF16)
        stored.append((state, normed, qkv, mixed, middle, normed_two, active, slope))
        state = (middle.astype(F32) + mul(active, down_w, NN) + bdown_f[layer]).astype(BF16)
    returned = to_slots(state)
    activations = jnp.where(live_mask, returned, jnp.zeros_like(returned))

    def reduce_all(array):
        array = lax.psum_scatter(array, ALL, scatter_dimension=0, tiled=True)
        return lax.all_gather(array, "dp", axis=0, tiled=False).astype(F32)

    upstream = grad.astype(F32)
    small_grads = [None] * LAYERS
    g_qkv, g_out, g_up, g_down = ([None] * LAYERS for _ in range(4))
    for layer in reversed(range(LAYERS)):
        qkv_t, out_w, up_t, down_w = weights[layer]
        state, normed, qkv, mixed, middle, normed_two, active, slope = stored[layer]
        low = upstream.astype(BF16)
        grad_b_down = jnp.sum(upstream, 0)
        grad_down = mul(active, low, TN).astype(BF16)
        grad_hidden = mul(low, down_w, NT) * slope.astype(F32)
        grad_b_up = jnp.sum(grad_hidden, 0)
        hidden_low = grad_hidden.astype(BF16)
        grad_up = mul(hidden_low, normed_two, TN).astype(BF16)
        two = jnp.concatenate(
            [
                grad_up.reshape(devices, up_rows, width),
                grad_down.reshape(devices, up_rows, width),
            ],
            axis=1,
        )
        two = reduce_all(two.reshape(devices * 2 * up_rows, width))
        g_up[layer] = two[:, :up_rows].reshape(ff_width, width).T
        g_down[layer] = two[:, up_rows:].reshape(ff_width, width)
        back, scale_two, shift_two = normalize_backward(
            middle, scale_f[layer, 1], mul(hidden_low, up_t, NN)
        )
        grad_middle = upstream + back
        grad_b_out = jnp.sum(grad_middle, 0)
        middle_low = grad_middle.astype(BF16)
        grad_out = mul(mixed, middle_low, TN).astype(BF16)
        grad_mixed = mul(middle_low, out_w, NT).astype(BF16)
        grad_qkv = attention_call(
            attention_backward_kernel, 3 * width, seq, length, qkv, grad_mixed
        )
        sums = jnp.sum(grad_qkv.astype(F32), 0)
        grad_b_qv = jnp.stack([sums[:width], sums[2 * width :]])
        grad_qkv_t = mul(grad_qkv, normed, TN).astype(BF16)
        one = jnp.concatenate(
            [
                grad_qkv_t.reshape(3, devices, head_rows, width)
                .transpose(1, 0, 2, 3)
                .reshape(devices, 3 * head_rows, width),
                grad_out.reshape(devices, head_rows, width),
            ],
            axis=1,
        )
        one = reduce_all(one.reshape(devices * 4 * head_rows, width))
        g_qkv[layer] = (
            one[:, : 3 * head_rows]
            .reshape(n_dp, 3, head_rows, width)
            .transpose(1, 3, 0, 2)
            .reshape(3, width, feat_width)
        )
        g_out[layer] = one[:, 3 * head_rows :].reshape(feat_width, width)
        back, scale_one, shift_one = normalize_backward(
            state, scale_f[layer, 0], mul(grad_qkv, qkv_t, NN)
        )
        upstream = grad_middle + back
        small_grads[layer] = (
            jnp.stack([scale_one, scale_two]),
            jnp.stack([shift_one, shift_two]),
            grad_b_qv,
            grad_b_out,
            grad_b_up,
            grad_b_down,
        )
    grad_input = to_slots(upstream).astype(F32)

    members = [jnp.stack([entry[i] for entry in small_grads]) for i in range(6)]
    flat = jnp.concatenate([m.reshape(-1) for m in members])
    flat = lax.psum(flat, ALL)
    out, start = [], 0
    for m in members:
        piece = flat[start : start + m.size].reshape(m.shape)
        start += m.size
        size = m.shape[-1] // n_tensor
        out.append(lax.dynamic_slice_in_dim(piece, tensor_rank * size, size, m.ndim - 1))
    return (
        activations,
        grad_input,
        out[0],
        out[1],
        jnp.stack(g_qkv),
        out[2],
        jnp.stack(g_out),
        out[3],
        jnp.stack(g_up),
        out[4],
        jnp.stack(g_down),
        out[5],
    )


def solution(mesh):
    placed = (
        P("dp", None, "tensor"),
        P("dp", None, "tensor"),
        P("dp"),
        P(None, None, "tensor"),
        P(None, None, "tensor"),
        P(None, None, None, "tensor"),
        P(None, None, "tensor"),
        P(None, "tensor", None),
        P(None, "tensor"),
        P(None, None, "tensor"),
        P(None, "tensor"),
        P(None, "tensor", None),
        P(None, "tensor"),
    )
    return jax.shard_map(
        on_device,
        mesh=mesh,
        in_specs=placed,
        out_specs=(
            P("dp", None, "tensor"),
            P("dp", None, "tensor"),
            P(None, None, "tensor"),
            P(None, None, "tensor"),
            P(None, None, None, "tensor"),
            P(None, None, "tensor"),
            P(None, "tensor", None),
            P(None, "tensor"),
            P(None, None, "tensor"),
            P(None, "tensor"),
            P(None, "tensor", None),
            P(None, "tensor"),
        ),
        check_vma=False,
    )
```

time: 1640 us -> 1210 us (0.74)
  waiting for transfers between devices: 1020 us -> 826 us
  matrix products: 214 us -> 116 us
  blocking collectives: 115 us -> 45 us
  other arithmetic: 111 us -> 46.6 us
  local copies, waits for them, and re-layouts: 148 us -> 94.5 us
  Pallas kernels: 0 us -> 39.4 us
  starting transfers between devices: 1.32 us -> 19.6 us
    all_gather x8, waiting for transfers between devices: 478 us -> 272 us  [the longest x4 176 us: gather_all(): return lax.all_gather(part, ALL, axis=0, tiled=False)]
    psum x5 -> x0, blocking collectives: 94.3 us -> none  [the longest x4 69.9 us: norm_backward(): lax.psum((jnp.sum(gained, -1), jnp.sum(gained * own_unit, -1)), 'tensor')]
    dot_general x34 -> x24, matrix products: 209 us -> 116 us  [mul(): return lax.dot_general(left, right, form, preferred_element_type=F32)]
    all_to_all x0 -> x4, waiting for transfers between devices: none -> 53.6 us  [the longest x2 35.1 us: to_images(): array = lax.all_to_all(array, 'tensor', 0, 0)]
    psum x1, waiting for transfers between devices: 142 us -> 96.9 us  [on_device(): flat = lax.psum(flat, ALL)]
    all_gather x0 -> x1, blocking collectives: none -> 45 us  [on_device(): flat = lax.all_gather(flat, 'tensor', axis=0, tiled=False).astype(F32)]
    pallas_call x0 -> x4, Pallas kernels: none -> 39.4 us  [attention_call(): pl.pallas_call(functools.partial(kernel, length=length), grid=(rows // se...]
    slice x6 -> x34, local copies, waits for them, and re-layouts: 7.81 us -> 43.6 us  [the longest x2 14.7 us: on_device(): two[:, up_rows:].reshape(devices * up_rows, width)]
  transfers between devices with their start and end apart: 17 -> 17, of which waited for: 17 -> 14; matrix products, arithmetic and copies ran while one was open for 5% -> 14% of each run, Pallas kernels for 0% -> 2%
where the time goes in v1:
time: 1210 us; the launch traced here: 1200 us
  waiting for transfers between devices  826 us (68%)
  matrix products  116 us (10%)
  local copies, waits for them, and re-layouts  94.5 us (8%)
  other arithmetic  46.6 us (4%)
  blocking collectives  45 us (4%)
  Pallas kernels  39.4 us (3%)
  starting transfers between devices  19.6 us (2%)
  between operations  16.4 us (1%)
    reduce_scatter x4, waiting for transfers between devices, reduce_all(): array = lax.psum_scatter(array, ALL, scatter_dimension=0, tiled=True)  403 us
    all_gather x4, waiting for transfers between devices, gather_all(): return lax.all_gather(part, ALL, axis=0, tiled=False)  176 us
    dot_general x24, matrix products, mul(): return lax.dot_general(left, right, form, preferred_element_type=F32)  116 us
    psum x1, waiting for transfers between devices, on_device(): flat = lax.psum(flat, ALL)  96.9 us
    all_gather x4, waiting for transfers between devices, reduce_all(): return lax.all_gather(array, 'dp', axis=0, tiled=False).astype(F32)  95.5 us
    all_gather x1, blocking collectives, on_device(): flat = lax.all_gather(flat, 'tensor', axis=0, tiled=False).astype(F32)  45 us
    pallas_call x4, Pallas kernels, attention_call(): pl.pallas_call(functools.partial(kernel, length=length), grid=(rows // se...  39.4 us
    all_to_all x2, waiting for transfers between devices, to_images(): array = lax.all_to_all(array, 'tensor', 0, 0)  35.1 us
  transfers between devices with their start and end apart: 17, of which 14 were waited for; matrix products, arithmetic and copies ran while one was open for 14% of the time, Pallas kernels for 2%

profile of v1, /device:TPU:0, one launch (start us, length us, event | category | flops | bytes accessed | tf_op | source)
XLA Modules:
  0.0 1202.8 jit_solution(9594149052897997867)
XLA Ops:
  9.0 2.6 fusion.111
  23.4 6.3 all-to-all-start.2
  31.0 35.1 %all-to-all-done.2 = bf16[4,3,197,192]{2,3,1,0:T(8,128)(2,1)S(1)} async-done(((bf16[4,3,197,192]{2,3,1,0:T(8,128)(2,1)}), bf16[4,3,197,192]{2,3,1,0:T(8,128)(2,1)S(1)}, u32[]{:S(2)}, u32[]{:S(2)}) %all-to-all-start.2) | async-done | bytes 907808 | tf_op jit(solution)/shard_map/all_to_all | solution.py:148
  66.1 4.3 all-to-all-start
  72.2 45.0 %all-gather.9 = bf16[4,1,4608]{2,1,0:T(2,128)(2,1)S(1)} all-gather(bf16[1,1,4608]{2,1,0:T(2,128)(2,1)S(1)} %reshape.489), channel_id=2, replica_groups=mesh['dp'=8,'tensor'=4] {'tensor'}, dimensions={0}, use_global_device_ids=true | all-gather | bytes 46080 | tf_op jit(solution)/shard_map/all_gather | solution.py:159
  126.3 2.6 copy.58
  135.2 2.4 slice.337
  137.6 2.2 slice.334
  139.8 33.8 %all-gather.19.cloned.1.call-done = bf16[3072,768]{1,0:T(8,128)(2,1)} async-done(((bf16[96,768]{1,0:T(8,128)(2,1)}), bf16[3072,768]{1,0:T(8,128)(2,1)}) %all-gather.19.cloned.1.call-update) | async-done | bytes 4718608 | tf_op jit(solution)/shard_map/all_gather | solution.py:114
  174.9 2.7 slice.317
  177.6 2.0 copy.64
  181.7 2.4 add_convert_fusion.1.qkv_ref
  184.1 5.7 shard_map.220
  191.5 66.4 %all-gather.25.cloned.1.call-done = bf16[6144,768]{1,0:T(8,128)(2,1)} async-done(((bf16[192,768]{1,0:T(8,128)(2,1)}), bf16[6144,768]{1,0:T(8,128)(2,1)}) %all-gather.25.cloned.1.call-update) | async-done | bytes 9437200 | tf_op jit(solution)/shard_map/all_gather | solution.py:114
  257.8 8.1 fusion.105
  265.9 75.9 %all-gather.21.cloned.1.call-done = bf16[6144,768]{1,0:T(8,128)(2,1)} async-done(((bf16[192,768]{1,0:T(8,128)(2,1)}), bf16[6144,768]{1,0:T(8,128)(2,1)}) %all-gather.21.cloned.1.call-update) | async-done | bytes 9437200 | tf_op jit(solution)/shard_map/all_gather | solution.py:114
  341.8 6.6 fusion.106
  348.5 6.9 multiply_convert_fusion.1
  355.4 3.3 convert_reduce_fusion.3
  359.2 2.6 add_convert_fusion.qkv_ref
  361.8 5.5 shard_map.221
  369.0 5.9 fusion.88
  374.9 11.2 fusion.10
  386.1 7.9 fusion.38
  397.2 14.2 %shard_map.222 = bf16[624,2304]{1,0:T(8,128)(2,1)S(1)} custom-call(bf16[624,2304]{1,0:T(8,128)(2,1)S(1)} %add_convert_fusion.qkv_ref, bf16[624,768]{1,0:T(8,128)(2,1)S(1)} %convolution_convert_fusion.9.grad_ref), custom_call_target="tpu_custom_call" | custom-call | flops 996802560 | bytes 6709248 | tf_op jit(solution)/shard_map/pallas_call | solution.py:66
  411.4 3.6 convolution_convert_fusion.4
  415.3 2.7 pad_maximum_fusion.3
  418.1 5.2 fusion.46
  424.1 9.5 fusion.12
  433.7 3.6 fusion.54
  441.4 14.0 %shard_map.223 = bf16[624,2304]{1,0:T(8,128)(2,1)S(1)} custom-call(bf16[624,2304]{1,0:T(8,128)(2,1)S(1)} %copy-done.2, bf16[624,768]{1,0:T(8,128)(2,1)S(1)} %convolution_convert_fusion.8.grad_ref), custom_call_target="tpu_custom_call" | custom-call | flops 996802560 | bytes 6709248 | tf_op jit(solution)/shard_map/pallas_call | solution.py:66
  455.4 3.7 convolution_convert_fusion.5
  461.5 2.8 pad_maximum_fusion.2
  464.4 7.4 convolution_convert_fusion.2
  471.8 7.7 convolution_convert_fusion.3
  479.5 4.0 pad_maximum_fusion
  483.8 6.4 convolution_convert_fusion
  490.2 7.8 convolution_convert_fusion.1
  498.0 4.0 pad_maximum_fusion.1
  503.8 7.6 fusion.96
  511.6 2.3 convert_reduce_fusion.1
  515.4 8.4 reduce-scatter.7.cloned.1.call-done
  523.8 112.9 %reduce-scatter.5.cloned.1.call-done = bf16[96,768]{1,0:T(8,128)(2,1)} async-done(((bf16[3072,768]{1,0:T(8,128)(2,1)}), bf16[96,768]{1,0:T(8,128)(2,1)}) %reduce-scatter.5.cloned.1.call-update) | async-done | bytes 147472 | tf_op jit(solution)/shard_map/reduce_scatter | solution.py:218
  636.8 140.4 %reduce-scatter.9.cloned.1.call-done = bf16[192,768]{1,0:T(8,128)(2,1)} async-done(((bf16[6144,768]{1,0:T(8,128)(2,1)}), bf16[192,768]{1,0:T(8,128)(2,1)}) %reduce-scatter.9.cloned.1.call-update) | async-done | bytes 294928 | tf_op jit(solution)/shard_map/reduce_scatter | solution.py:218
  777.4 141.6 %reduce-scatter.11.cloned.1.call-done = bf16[192,768]{1,0:T(8,128)(2,1)} async-done(((bf16[6144,768]{1,0:T(8,128)(2,1)}), bf16[192,768]{1,0:T(8,128)(2,1)}) %reduce-scatter.11.cloned.1.call-update) | async-done | bytes 294928 | tf_op jit(solution)/shard_map/reduce_scatter | solution.py:218
  919.0 6.8 fusion.61
  928.5 3.6 copy.66
  932.0 4.3 all-to-all-start.1
  936.4 3.1 add_convert_fusion.3
  939.5 3.1 reshape.447
  943.0 2.1 copy.68
  945.1 18.5 %all-to-all-done.1 = bf16[4,3,197,192]{2,3,1,0:T(8,128)(2,1)} async-done(((bf16[4,3,197,192]{2,3,1,0:T(8,128)(2,1)}), bf16[4,3,197,192]{2,3,1,0:T(8,128)(2,1)}, u32[]{:S(2)}, u32[]{:S(2)}) %all-to-all-start.1) | async-done | bytes 907808 | tf_op jit(solution)/shard_map/all_to_all | solution.py:154
  963.6 3.8 all-to-all-start.3
  967.4 96.9 %all-reduce.6.cloned.1.call-done = f32[18432]{0:T(1024)} async-done(((f32[18432]{0:T(1024)}), f32[18432]{0:T(1024)}) %all-reduce.6.cloned.1.call-update) | async-done | bytes 73744 | tf_op jit(solution)/shard_map/psum | solution.py:291
  1070.5 2.3 slice_select_fusion
  1074.2 17.8 %all-gather.29.cloned.1.call-done = bf16[768,768]{1,0:T(8,128)(2,1)} async-done(((bf16[96,768]{1,0:T(8,128)(2,1)}), bf16[768,768]{1,0:T(8,128)(2,1)}) %all-gather.29.cloned.1.call-update) | async-done | bytes 1179664 | tf_op jit(solution)/shard_map/all_gather | solution.py:219
  1093.5 24.5 %all-gather.27.cloned.1.call-done = bf16[768,768]{1,0:T(8,128)(2,1)} async-done(((bf16[96,768]{1,0:T(8,128)(2,1)}), bf16[768,768]{1,0:T(8,128)(2,1)}) %all-gather.27.cloned.1.call-update) | async-done | bytes 1179664 | tf_op jit(solution)/shard_map/all_gather | solution.py:219
  1122.9 25.9 %all-gather.31.cloned.1.call-done = bf16[1536,768]{1,0:T(8,128)(2,1)} async-done(((bf16[192,768]{1,0:T(8,128)(2,1)}), bf16[1536,768]{1,0:T(8,128)(2,1)}) %all-gather.31.cloned.1.call-update) | async-done | bytes 2359312 | tf_op jit(solution)/shard_map/all_gather | solution.py:219
  1148.7 3.5 fusion.107
  1152.2 27.4 %all-gather.33.cloned.1.call-done = bf16[1536,768]{1,0:T(8,128)(2,1)} async-done(((bf16[192,768]{1,0:T(8,128)(2,1)}), bf16[1536,768]{1,0:T(8,128)(2,1)}) %all-gather.33.cloned.1.call-update) | async-done | bytes 2359312 | tf_op jit(solution)/shard_map/all_gather | solution.py:219
  1179.7 3.7 fusion.108
  1183.3 2.5 pad_maximum_fusion.4
  1185.8 6.0 copy.73
  1191.9 4.2 pad_maximum_fusion.5
  (354 shorter events, 69.6 us)
Async XLA Ops:
  7.2 128.0 %all-gather.23.cloned.1.call-start = ((), (), s32[]{:S(2)}) async-start(), calls=%async_computation.15 | async-start | bytes 4866048 | tf_op jit(solution)/shard_map/all_gather | solution.py:114
  9.0 5.8 copy-start.28
  13.3 160.3 %all-gather.19.cloned.1.call-start = ((), (), s32[]{:S(2)}) async-start(), calls=%async_computation.13 | async-start | bytes 4866048 | tf_op jit(solution)/shard_map/all_gather | solution.py:114
  14.8 243.1 %all-gather.25.cloned.1.call-start = ((), (), s32[]{:S(2)}) async-start(), calls=%async_computation.16 | async-start | bytes 9732096 | tf_op jit(solution)/shard_map/all_gather | solution.py:114
  18.6 323.3 %all-gather.21.cloned.1.call-start = ((), (), s32[]{:S(2)}) async-start(), calls=%async_computation.14 | async-start | bytes 9732096 | tf_op jit(solution)/shard_map/all_gather | solution.py:114
  22.2 7.5 copy-start.33
  23.4 42.7 %all-to-all-start.2 = ((bf16[4,3,197,192]{2,3,1,0:T(8,128)(2,1)}), bf16[4,3,197,192]{2,3,1,0:T(8,128)(2,1)S(1)}, u32[]{:S(2)}, u32[]{:S(2)}) async-start(bf16[4,3,197,192]{2,3,1,0:T(8,128)(2,1)} %bitcast.45), calls=%async_computation.2 | async-start | bytes 2359296 | tf_op jit(solution)/shard_map/all_to_all | solution.py:148
  29.7 40.7 %copy-start.60 = (bf16[2,192]{1,0:T(2,128)(2,1)S(1)}, bf16[2,192]{1,0:T(2,128)(2,1)}, u32[]{:S(2)}) copy-start(bf16[2,192]{1,0:T(2,128)(2,1)} %param.21) | copy-start | bytes 2308
  29.7 40.8 %copy-start.61 = (bf16[2,192]{1,0:T(2,128)(2,1)S(1)}, bf16[2,192]{1,0:T(2,128)(2,1)}, u32[]{:S(2)}) copy-start(bf16[2,192]{1,0:T(2,128)(2,1)} %param.25) | copy-start | bytes 2308
  29.7 40.9 %copy-start.57 = (bf16[2,2,192]{2,1,0:T(2,128)(2,1)S(1)}, bf16[2,2,192]{2,1,0:T(2,128)(2,1)}, u32[]{:S(2)}) copy-start(bf16[2,2,192]{2,1,0:T(2,128)(2,1)} %param.16) | copy-start | bytes 4612
  29.7 40.9 %copy-start.58 = (bf16[2,2,192]{2,1,0:T(2,128)(2,1)S(1)}, bf16[2,2,192]{2,1,0:T(2,128)(2,1)}, u32[]{:S(2)}) copy-start(bf16[2,2,192]{2,1,0:T(2,128)(2,1)} %param.17) | copy-start | bytes 4612
  29.8 41.0 %copy-start.59 = (bf16[2,2,192]{2,1,0:T(2,128)(2,1)S(1)}, bf16[2,2,192]{2,1,0:T(2,128)(2,1)}, u32[]{:S(2)}) copy-start(bf16[2,2,192]{2,1,0:T(2,128)(2,1)} %param.19) | copy-start | bytes 4612
  29.8 41.1 %copy-start.54 = (bf16[2,768]{1,0:T(2,128)(2,1)S(1)}, bf16[2,768]{1,0:T(2,128)(2,1)}, u32[]{:S(2)}) copy-start(bf16[2,768]{1,0:T(2,128)(2,1)} %param.23) | copy-start | bytes 9220
  66.1 60.1 %all-to-all-start = ((bf16[4,3,197,192]{2,3,1,0:T(8,128)(2,1)}), bf16[4,3,197,192]{2,3,1,0:T(8,128)(2,1)}, u32[]{:S(2)}, u32[]{:S(2)}) async-start(bf16[4,3,197,192]{2,3,1,0:T(8,128)(2,1)} %bitcast.1), calls=%async_computation | async-start | bytes 2359296 | tf_op jit(solution)/shard_map/all_to_all | solution.py:148
  70.4 453.4 %reduce-scatter.7.cloned.1.call-start = ((), (), s32[]{:S(2)}) async-start(), calls=%async_computation.10 | async-start | bytes 4866048 | tf_op jit(solution)/shard_map/reduce_scatter | solution.py:218
  174.9 14.9 %copy-start.30 = (bf16[32,24,768]{2,1,0:T(8,128)(2,1)}, bf16[32,24,768]{2,1,0:T(8,128)(2,1)S(1)}, u32[]{:S(2)}) copy-start(bf16[32,24,768]{2,1,0:T(8,128)(2,1)S(1)} %slice.321) | copy-start | bytes 3538948
  184.1 5.7 copy-start.1
  184.1 5.7 copy-start.34
  184.1 5.7 copy-start.53
  190.8 164.6 %copy-start.8 = (bf16[624,768]{1,0:T(8,128)(2,1)}, bf16[624,768]{1,0:T(8,128)(2,1)S(1)}, u32[]{:S(2)}) copy-start(bf16[624,768]{1,0:T(8,128)(2,1)S(1)} %fusion.70) | copy-start | bytes 2875396
  341.8 6.6 copy-start.44
  341.8 6.6 copy-start.49
  348.4 6.9 copy-start.19
  348.4 6.9 copy-start.20
  348.4 6.9 copy-start.52
  355.4 3.8 copy-start.27
  355.4 3.8 copy-start.46
  355.4 13.5 %slice-start.4 = ((s8[4718592]{0:T(1024)(128)(4,1)}), s8[4194304]{0:T(1024)(128)(4,1)S(1)}, s32[]{:S(2)}) async-start(s8[4718592]{0:T(1024)(128)(4,1)} %bitcast.217), calls=%async_computation.25 | async-start | bytes 8388608
  358.7 52.7 %copy-start.21 = (bf16[624,768]{1,0:T(8,128)(2,1)}, bf16[624,768]{1,0:T(8,128)(2,1)S(1)}, u32[]{:S(2)}) copy-start(bf16[624,768]{1,0:T(8,128)(2,1)S(1)} %get-tuple-element.130) | copy-start | bytes 2875396
  358.7 10.2 slice-start.5
  361.8 5.5 copy-start.32
  361.8 5.5 copy-start.51
  367.4 7.5 slice-start
  368.4 25.5 %copy-start.23 = (bf16[624,768]{1,0:T(8,128)(2,1)}, bf16[624,768]{1,0:T(8,128)(2,1)S(1)}, u32[]{:S(2)}) copy-start(bf16[624,768]{1,0:T(8,128)(2,1)S(1)} %get-tuple-element.132) | copy-start | bytes 2875396
  368.9 5.9 slice-start.1
  368.9 5.9 copy-start.25
  368.9 5.9 copy-start.45
  418.0 218.7 %reduce-scatter.5.cloned.1.call-start = ((), (), s32[]{:S(2)}) async-start(), calls=%async_computation.9 | async-start | bytes 4866048 | tf_op jit(solution)/shard_map/reduce_scatter | solution.py:218
  418.1 5.2 copy-start.16
  418.1 5.2 copy-start.22
  423.3 10.3 slice-start.2
  424.1 13.9 %copy-start.14 = (f32[624,768]{1,0:T(8,128)}, f32[624,768]{1,0:T(8,128)S(1)}, u32[]{:S(2)}) copy-start(f32[624,768]{1,0:T(8,128)S(1)} %get-tuple-element.83) | copy-start | bytes 5750788
  424.1 9.5 copy-start.9
  424.1 9.5 slice-start.3
  433.6 4.4 copy-start.64
  438.8 20.6 %copy-start.12 = (f32[624,768]{1,0:T(8,128)}, f32[624,768]{1,0:T(8,128)S(1)}, u32[]{:S(2)}) copy-start(f32[624,768]{1,0:T(8,128)S(1)} %get-tuple-element.89) | copy-start | bytes 5750788
  441.4 14.0 %copy-start.29 = (f32[624,768]{1,0:T(8,128)S(1)}, f32[624,768]{1,0:T(8,128)}, u32[]{:S(2)}) copy-start(f32[624,768]{1,0:T(8,128)} %fusion.69) | copy-start | bytes 5750788
  464.3 312.9 %reduce-scatter.9.cloned.1.call-start = ((), (), s32[]{:S(2)}) async-start(), calls=%async_computation.11 | async-start | bytes 9732096 | tf_op jit(solution)/shard_map/reduce_scatter | solution.py:218
  464.3 7.4 copy-start.10
  464.3 7.4 copy-start.65
  483.5 435.4 %reduce-scatter.11.cloned.1.call-start = ((), (), s32[]{:S(2)}) async-start(), calls=%async_computation.12 | async-start | bytes 9732096 | tf_op jit(solution)/shard_map/reduce_scatter | solution.py:218
  483.7 6.4 copy-start.24
  483.7 6.4 copy-start.63
  502.0 562.3 %all-reduce.6.cloned.1.call-start = ((), (), s32[]{:S(2)}) async-start(), calls=%async_computation.8 | async-start | bytes 147456 | tf_op jit(solution)/shard_map/psum | solution.py:291
  514.0 263.3 %copy-start.42 = (f32[4,192]{1,0:T(4,128)S(1)}, f32[4,192]{1,0:T(4,128)}, u32[]{:S(2)}) copy-start(f32[4,192]{1,0:T(4,128)} %get-tuple-element.78) | copy-start | bytes 9220
  515.3 576.6 %all-gather.29.cloned.1.call-start = ((), (), s32[]{:S(2)}) async-start(), calls=%async_computation.18 | async-start | bytes 1327104 | tf_op jit(solution)/shard_map/all_gather | solution.py:219
  523.8 594.2 %all-gather.27.cloned.1.call-start = ((), (), s32[]{:S(2)}) async-start(), calls=%async_computation.17 | async-start | bytes 1327104 | tf_op jit(solution)/shard_map/all_gather | solution.py:219
  636.7 512.0 %all-gather.31.cloned.1.call-start = ((), (), s32[]{:S(2)}) async-start(), calls=%async_computation.19 | async-start | bytes 2654208 | tf_op jit(solution)/shard_map/all_gather | solution.py:219
  777.2 402.4 %all-gather.33.cloned.1.call-start = ((), (), s32[]{:S(2)}) async-start(), calls=%async_computation.20 | async-start | bytes 2654208 | tf_op jit(solution)/shard_map/all_gather | solution.py:219
  928.5 7.9 copy-start.6
  928.5 7.9 copy-start.13
  932.0 31.6 %all-to-all-start.1 = ((bf16[4,3,197,192]{2,3,1,0:T(8,128)(2,1)}), bf16[4,3,197,192]{2,3,1,0:T(8,128)(2,1)}, u32[]{:S(2)}, u32[]{:S(2)}) async-start(bf16[4,3,197,192]{2,3,1,0:T(8,128)(2,1)} %copy.66), calls=%async_computation.1 | async-start | bytes 2359296 | tf_op jit(solution)/shard_map/all_to_all | solution.py:154
  945.1 125.4 %copy-start.56 = (pred[10]{0:T(512)(128)(4,1)S(1)}, pred[10]{0:T(512)(128)(4,1)}, u32[]{:S(2)}) copy-start(pred[10]{0:T(512)(128)(4,1)} %copy-done.55) | copy-start | bytes 34
  963.6 109.2 %all-to-all-start.3 = ((bf16[4,3,197,192]{2,3,1,0:T(8,128)(2,1)}), bf16[4,3,197,192]{2,3,1,0:T(8,128)(2,1)S(1)}, u32[]{:S(2)}, u32[]{:S(2)}) async-start(bf16[4,3,197,192]{2,3,1,0:T(8,128)(2,1)} %copy.68), calls=%async_computation.3 | async-start | bytes 2359296 | tf_op jit(solution)/shard_map/all_to_all | solution.py:154
  (26 other events, 54.3 us)
Sparse Core Ops, SparseCore 0:
  13.4 88.6 all-gather.22
  105.0 68.5 all-gather.18
  177.1 80.7 all-gather.24
  261.2 80.6 all-gather.20
  418.1 105.5 reduce-scatter.6
  530.6 106.1 reduce-scatter.4
  642.6 134.5 reduce-scatter.8
  784.1 134.8 reduce-scatter.10
  924.6 139.6 all-reduce.5
  1066.0 25.9 all-gather.28
  1093.8 24.0 all-gather.26
  1119.7 29.0 all-gather.30
  1150.6 29.0 all-gather.32

commit v2 on v1

--- a/solution.py
+++ b/solution.py
@@ -108,10 +108,6 @@
 def own_rows(matrix, rank, parts):
     size = matrix.shape[-2] // parts
     return lax.dynamic_slice_in_dim(matrix, rank * size, size, matrix.ndim - 2)
-
-
-def gather_all(part):
-    return lax.all_gather(part, ALL, axis=0, tiled=False)
 
 
 def on_device(
@@ -134,7 +130,6 @@
     n_tensor = lax.axis_size("tensor")
     devices = n_dp * n_tensor
     dp_rank = lax.axis_index("dp")
-    tensor_rank = lax.axis_index("tensor")
     width = feat_width * n_tensor
     ff_width = w_up.shape[-1]
     each = -(-slot_count // n_tensor)
@@ -154,45 +149,52 @@
         array = lax.all_to_all(array.transpose(2, 0, 1, 3), "tensor", 0, 0)
         return array.reshape(each * n_tensor, length, feat_width)[:slot_count]
 
+    head_rows = feat_width // n_dp
+    up_rows = ff_width // n_dp
+    used_rows = 4 * head_rows + 2 * up_rows
+    slab_rows = -(-(used_rows + 1) // 16) * 16
+
     small = [ln_scale, ln_shift, b_qv, b_out, b_up, b_down]
     flat = jnp.concatenate([a.reshape(-1) for a in small])
-    flat = lax.all_gather(flat, "tensor", axis=0, tiled=False).astype(F32)
+    share = flat.size // n_dp
+    extra = lax.dynamic_slice_in_dim(flat, dp_rank * share, share, 0)
+    weights = []
+    for layer in range(LAYERS):
+        slab = jnp.concatenate(
+            [
+                own_slice(w_qkv[layer], dp_rank, n_dp).reshape(3 * head_rows, width),
+                own_rows(w_out[layer], dp_rank, n_dp),
+                own_slice(w_up[layer], dp_rank, n_dp),
+                own_rows(w_down[layer], dp_rank, n_dp),
+            ]
+        )
+        if layer == 0:
+            last = jnp.pad(extra, (0, width - share))[None]
+            slab = jnp.concatenate([slab, last])
+        else:
+            slab, gathered = lax.optimization_barrier((slab, gathered))
+        slab = jnp.pad(slab, ((0, slab_rows - slab.shape[0]), (0, 0)))
+        gathered = lax.all_gather(slab, ALL, axis=0, tiled=False)
+        if layer == 0:
+            flat = gathered[:, used_rows, :share].reshape(n_tensor, n_dp * share).astype(F32)
+        at = 4 * head_rows
+        weights.append(
+            (
+                gathered[:, : 3 * head_rows]
+                .reshape(devices, 3, head_rows, width)
+                .transpose(1, 0, 2, 3)
+                .reshape(3 * width, width),
+                gathered[:, 3 * head_rows : at].reshape(width, width),
+                gathered[:, at : at + up_rows].reshape(devices * up_rows, width),
+                gathered[:, at + up_rows : used_rows].reshape(devices * up_rows, width),
+            )
+        )
     full, start = [], 0
     for a in small:
         piece = flat[:, start : start + a.size].reshape((n_tensor,) + a.shape)
         start += a.size
         full.append(jnp.moveaxis(piece, 0, -2).reshape(a.shape[:-1] + (n_tensor * a.shape[-1],)))
     scale_f, shift_f, bqv_f, bout_f, bup_f, bdown_f = full
-
-    head_rows = feat_width // n_dp
-    up_rows = ff_width // n_dp
-    weights = []
-    for layer in range(LAYERS):
-        one = jnp.concatenate(
-            [
-                own_slice(w_qkv[layer], dp_rank, n_dp).reshape(3 * head_rows, width),
-                own_rows(w_out[layer], dp_rank, n_dp),
-            ]
-        )
-        two = jnp.concatenate(
-            [own_slice(w_up[layer], dp_rank, n_dp), own_rows(w_down[layer], dp_rank, n_dp)]
-        )
-        one = gather_all(one)
-        two = gather_all(two)
-        qkv_t = (
-            one[:, : 3 * head_rows]
-            .reshape(devices, 3, head_rows, width)
-            .transpose(1, 0, 2, 3)
-            .reshape(3 * width, width)
-        )
-        weights.append(
-            (
-                qkv_t,
-                one[:, 3 * head_rows :].reshape(width, width),
-                two[:, :up_rows].reshape(devices * up_rows, width),
-                two[:, up_rows:].reshape(devices * up_rows, width),
-            )
-        )
 
     state = to_images(tokens)
     grad = to_images(jnp.where(live_mask, cotangent, jnp.zeros_like(cotangent)))
@@ -214,13 +216,8 @@
     returned = to_slots(state)
     activations = jnp.where(live_mask, returned, jnp.zeros_like(returned))
 
-    def reduce_all(array):
-        array = lax.psum_scatter(array, ALL, scatter_dimension=0, tiled=True)
-        return lax.all_gather(array, "dp", axis=0, tiled=False).astype(F32)
-
     upstream = grad.astype(F32)
-    small_grads = [None] * LAYERS
-    g_qkv, g_out, g_up, g_down = ([None] * LAYERS for _ in range(4))
+    summed = [None] * LAYERS
     for layer in reversed(range(LAYERS)):
         qkv_t, out_w, up_t, down_w = weights[layer]
         state, normed, qkv, mixed, middle, normed_two, active, slope = stored[layer]
@@ -231,16 +228,6 @@
         grad_b_up = jnp.sum(grad_hidden, 0)
         hidden_low = grad_hidden.astype(BF16)
         grad_up = mul(hidden_low, normed_two, TN).astype(BF16)
-        two = jnp.concatenate(
-            [
-                grad_up.reshape(devices, up_rows, width),
-                grad_down.reshape(devices, up_rows, width),
-            ],
-            axis=1,
-        )
-        two = reduce_all(two.reshape(devices * 2 * up_rows, width))
-        g_up[layer] = two[:, :up_rows].reshape(ff_width, width).T
-        g_down[layer] = two[:, up_rows:].reshape(ff_width, width)
         back, scale_two, shift_two = normalize_backward(
             middle, scale_f[layer, 1], mul(hidden_low, up_t, NN)
         )
@@ -255,58 +242,84 @@
         sums = jnp.sum(grad_qkv.astype(F32), 0)
         grad_b_qv = jnp.stack([sums[:width], sums[2 * width :]])
         grad_qkv_t = mul(grad_qkv, normed, TN).astype(BF16)
-        one = jnp.concatenate(
-            [
-                grad_qkv_t.reshape(3, devices, head_rows, width)
-                .transpose(1, 0, 2, 3)
-                .reshape(devices, 3 * head_rows, width),
-                grad_out.reshape(devices, head_rows, width),
-            ],
-            axis=1,
-        )
-        one = reduce_all(one.reshape(devices * 4 * head_rows, width))
-        g_qkv[layer] = (
-            one[:, : 3 * head_rows]
-            .reshape(n_dp, 3, head_rows, width)
-            .transpose(1, 3, 0, 2)
-            .reshape(3, width, feat_width)
-        )
-        g_out[layer] = one[:, 3 * head_rows :].reshape(feat_width, width)
         back, scale_one, shift_one = normalize_backward(
             state, scale_f[layer, 0], mul(grad_qkv, qkv_t, NN)
         )
         upstream = grad_middle + back
-        small_grads[layer] = (
+        members = [
             jnp.stack([scale_one, scale_two]),
             jnp.stack([shift_one, shift_two]),
             grad_b_qv,
             grad_b_out,
             grad_b_up,
             grad_b_down,
+        ]
+        flat = jnp.concatenate(
+            [
+                jnp.moveaxis(m.reshape(m.shape[:-1] + (n_tensor, -1)), -2, 0).reshape(n_tensor, -1)
+                for m in members
+            ],
+            axis=1,
+        )
+        flat = flat.astype(BF16).reshape(devices, 1, -1)
+        part = flat.shape[-1]
+        slab = jnp.concatenate(
+            [
+                grad_qkv_t.reshape(3, devices, head_rows, width)
+                .transpose(1, 0, 2, 3)
+                .reshape(devices, 3 * head_rows, width),
+                grad_out.reshape(devices, head_rows, width),
+                grad_up.reshape(devices, up_rows, width),
+                grad_down.reshape(devices, up_rows, width),
+                jnp.pad(
+                    flat, ((0, 0), (0, slab_rows - used_rows - 1), (0, width - part))
+                ),
+            ],
+            axis=1,
+        )
+        if layer < LAYERS - 1:
+            slab, summed[layer + 1] = lax.optimization_barrier((slab, summed[layer + 1]))
+        summed[layer] = lax.psum_scatter(
+            slab.reshape(devices * slab_rows, width), ALL, scatter_dimension=0, tiled=True
         )
     grad_input = to_slots(upstream).astype(F32)
 
-    members = [jnp.stack([entry[i] for entry in small_grads]) for i in range(6)]
-    flat = jnp.concatenate([m.reshape(-1) for m in members])
-    flat = lax.psum(flat, ALL)
+    total = lax.all_gather(jnp.stack(summed), "dp", axis=0, tiled=False)
+    at = 4 * head_rows
+    g_qkv = (
+        total[:, :, : 3 * head_rows]
+        .reshape(n_dp, LAYERS, 3, head_rows, width)
+        .transpose(1, 2, 4, 0, 3)
+        .reshape(LAYERS, 3, width, feat_width)
+        .astype(F32)
+    )
+
+    def by_rows(piece):
+        return jnp.swapaxes(piece, 0, 1).reshape(LAYERS, -1, width).astype(F32)
+
+    g_out = by_rows(total[:, :, 3 * head_rows : at])
+    g_up = jnp.swapaxes(by_rows(total[:, :, at : at + up_rows]), 1, 2)
+    g_down = by_rows(total[:, :, at + up_rows : used_rows])
+    flat = jnp.swapaxes(total[:, :, used_rows, :part], 0, 1).reshape(LAYERS, -1).astype(F32)
     out, start = [], 0
     for m in members:
-        piece = flat[start : start + m.size].reshape(m.shape)
-        start += m.size
-        size = m.shape[-1] // n_tensor
-        out.append(lax.dynamic_slice_in_dim(piece, tensor_rank * size, size, m.ndim - 1))
+        size = m.size // n_tensor
+        out.append(
+            flat[:, start : start + size].reshape((LAYERS,) + m.shape[:-1] + (m.shape[-1] // n_tensor,))
+        )
+        start += size
     return (
         activations,
         grad_input,
         out[0],
         out[1],
-        jnp.stack(g_qkv),
+        g_qkv,
         out[2],
-        jnp.stack(g_out),
+        g_out,
         out[3],
-        jnp.stack(g_up),
+        g_up,
         out[4],
-        jnp.stack(g_down),
+        g_down,
         out[5],
     )
 

time: 1210 us -> 855 us (0.71)
  waiting for transfers between devices: 826 us -> 475 us
  blocking collectives: 45 us -> 0 us
  local copies, waits for them, and re-layouts: 94.5 us -> 138 us
  matrix products: 116 us -> 131 us
  other arithmetic: 46.6 us -> 34.2 us
    reduce_scatter x4 -> x2, waiting for transfers between devices: 403 us -> 238 us  [on_device(): lax.psum_scatter(slab.reshape(devices * slab_rows, width), ALL, scatter_d...]
    all_gather x8 -> x3, waiting for transfers between devices: 272 us -> 115 us  [the longest x2 115 us: on_device(): gathered = lax.all_gather(slab, ALL, axis=0, tiled=False)]
    psum x1 -> x0, waiting for transfers between devices: 96.9 us -> none  [on_device(): flat = lax.psum(flat, ALL)]
    all_gather x1 -> x0, blocking collectives: 45 us -> none  [on_device(): flat = lax.all_gather(flat, 'tensor', axis=0, tiled=False).astype(F32)]
    all_to_all x2, waiting for transfers between devices: 35.1 us -> 77.6 us  [to_images(): array = lax.all_to_all(array, 'tensor', 0, 0)]
    all_to_all x2, waiting for transfers between devices: 18.5 us -> 44.6 us  [to_slots(): array = lax.all_to_all(array.transpose(2, 0, 1, 3), 'tensor', 0, 0)]
    unnamed x162 -> x195, local copies, waits for them, and re-layouts: 15.5 us -> 34.7 us
    dot_general x24, matrix products: 116 us -> 131 us  [mul(): return lax.dot_general(left, right, form, preferred_element_type=F32)]
  transfers between devices with their start and end apart: 17 -> 9, of which waited for: 14 -> 8; matrix products, arithmetic and copies ran while one was open for 14% -> 18% of each run, Pallas kernels for 2% -> 2%
where the time goes in v2:
time: 855 us; the launch traced here: 850 us
  waiting for transfers between devices  475 us (56%)
  local copies, waits for them, and re-layouts  138 us (16%)
  matrix products  131 us (15%)
  Pallas kernels  39.3 us (5%)
  other arithmetic  34.2 us (4%)
  between operations  16.1 us (2%)
  starting transfers between devices  15.5 us (2%)
    reduce_scatter x2, waiting for transfers between devices, on_device(): lax.psum_scatter(slab.reshape(devices * slab_rows, width), ALL, scatter_d...  238 us
    dot_general x24, matrix products, mul(): return lax.dot_general(left, right, form, preferred_element_type=F32)  131 us
    all_gather x2, waiting for transfers between devices, on_device(): gathered = lax.all_gather(slab, ALL, axis=0, tiled=False)  115 us
    all_to_all x2, waiting for transfers between devices, to_images(): array = lax.all_to_all(array, 'tensor', 0, 0)  77.6 us
    all_to_all x2, waiting for transfers between devices, to_slots(): array = lax.all_to_all(array.transpose(2, 0, 1, 3), 'tensor', 0, 0)  44.6 us
    pallas_call x4, Pallas kernels, attention_call(): pl.pallas_call(functools.partial(kernel, length=length), grid=(rows // se...  39.3 us
    unnamed x195, local copies, waits for them, and re-layouts  34.7 us
  transfers between devices with their start and end apart: 9, of which 8 were waited for; matrix products, arithmetic and copies ran while one was open for 18% of the time, Pallas kernels for 2%

profile of v2, /device:TPU:0, one launch (start us, length us, event | category | flops | bytes accessed | tf_op | source)
XLA Modules:
  0.0 849.5 jit_solution(769023399259666029)
XLA Ops:
  14.8 2.6 fusion.110
  28.9 108.3 %all-gather.7.cloned.1.call-done = bf16[9728,768]{1,0:T(8,128)(2,1)} async-done(((bf16[304,768]{1,0:T(8,128)(2,1)}), bf16[9728,768]{1,0:T(8,128)(2,1)}) %all-gather.7.cloned.1.call-update) | async-done | bytes 14942224 | tf_op jit(solution)/shard_map/all_gather | solution.py:177
  140.6 3.5 all-to-all-start.2
  145.3 38.0 %all-to-all-done.2 = bf16[4,3,197,192]{2,3,1,0:T(8,128)(2,1)S(1)} async-done(((bf16[4,3,197,192]{2,3,1,0:T(8,128)(2,1)}), bf16[4,3,197,192]{2,3,1,0:T(8,128)(2,1)S(1)}, u32[]{:S(2)}, u32[]{:S(2)}) %all-to-all-start.2) | async-done | bytes 907808 | tf_op jit(solution)/shard_map/all_to_all | solution.py:143
  183.3 3.5 all-to-all-start
  187.1 2.6 copy.80
  192.9 39.5 %all-to-all-done = bf16[4,3,197,192]{2,3,1,0:T(8,128)(2,1)S(1)} async-done(((bf16[4,3,197,192]{2,3,1,0:T(8,128)(2,1)}), bf16[4,3,197,192]{2,3,1,0:T(8,128)(2,1)S(1)}, u32[]{:S(2)}, u32[]{:S(2)}) %all-to-all-start) | async-done | bytes 907808 | tf_op jit(solution)/shard_map/all_to_all | solution.py:143
  237.0 4.5 slice.283
  244.4 2.2 copy.75
  248.5 2.4 add_convert_fusion.1.qkv_ref
  251.0 5.5 shard_map.220
  258.1 6.6 fusion.107
  264.8 7.1 multiply_convert_fusion.1
  271.9 3.3 convert_reduce_fusion.1
  275.7 6.2 all-gather.9.cloned.1.call-done
  281.9 2.4 slice.303
  284.3 2.2 slice.300
  286.5 6.6 fusion.106
  293.3 2.6 add_convert_fusion.qkv_ref
  296.0 5.5 shard_map.221
  303.0 5.5 fusion.89
  308.5 11.8 %fusion.10 = (bf16[3072]{0:T(1024)(128)(2,1)S(1)}, bf16[624,3072]{1,0:T(8,128)(2,1)}, bf16[624,3072]{1,0:T(8,128)(2,1)}, f32[624,3072]{1,0:T(8,128)}) fusion(f32[624,3072]{1,0:T(8,128)} %fusion.89, f32[3072]{0:T(1024)S(1)} %bitcast.233, bf16[624,768]{1,0:T(8,128)(2,1)S(1)} %bitcast.203, bf16[3072,768]{1,0:T(8,128)(2,1)S(1)} %bitcast.191), kind=kOutput, calls=%fused_computation.20 | convolution fusion | flops 2973152256 | bytes 28698624 | tf_op jit(solution)/shard_map/dot_general | solution.py:22
  320.3 8.0 fusion.38
  328.3 10.2 %convolution_convert_fusion.1 = bf16[3072,768]{1,0:T(8,128)(2,1)} fusion(bf16[624,768]{1,0:T(8,128)(2,1)S(1)} %get-tuple-element.138, f32[768]{0:T(1024)S(1)} %get-tuple-element.76, f32[768]{0:T(1024)S(1)} %get-tuple-element.72, f32[624]{0:T(1024)S(1)} %add_rsqrt_fusion, f32[624]{0:T(1024)S(1)} %broadcast_multiply_fusion.8, ...), kind=kOutput, calls=%fused_computation.25 | convolution fusion | flops 2955386880 | bytes 17189760 | tf_op jit(solution)/shard_map/dot_general | solution.py:22
  340.6 2.1 convolution_convert_fusion.6
  342.8 14.2 %shard_map.222 = bf16[624,2304]{1,0:T(8,128)(2,1)S(1)} custom-call(bf16[624,2304]{1,0:T(8,128)(2,1)S(1)} %add_convert_fusion.qkv_ref, bf16[624,768]{1,0:T(8,128)(2,1)S(1)} %convolution_convert_fusion.9.grad_ref), custom_call_target="tpu_custom_call" | custom-call | flops 996802560 | bytes 6709248 | tf_op jit(solution)/shard_map/pallas_call | solution.py:66
  357.0 4.5 fusion.46
  362.0 6.1 convolution_convert_fusion.4
  371.9 2.2 copy.87
  379.0 6.2 convolution_convert_fusion
  385.3 2.0 constant_dynamic-update-slice_fusion.9
  389.6 2.4 constant_dynamic-update-slice_fusion.7
  392.0 2.5 constant_dynamic-update-slice_fusion.6
  398.3 2.5 fusion.101
  400.9 12.2 %fusion.12 = (bf16[3072]{0:T(1024)(128)(2,1)S(1)}, bf16[624,3072]{1,0:T(8,128)(2,1)}, f32[624,3072]{1,0:T(8,128)}) fusion(f32[624,3072]{1,0:T(8,128)} %get-tuple-element.134, f32[3072]{0:T(1024)S(1)} %bitcast.232, bf16[3072,768]{1,0:T(8,128)(2,1)} %bitcast.195, f32[624,768]{1,0:T(8,128)S(1)} %get-tuple-element.93), kind=kOutput, calls=%fused_computation.22 | convolution fusion | flops 2969797632 | bytes 25823232 | tf_op jit(solution)/shard_map/dot_general | solution.py:22
  413.8 11.3 %fusion.54 = (bf16[768]{0:T(1024)(128)(2,1)S(1)}, f32[624]{0:T(1024)S(1)}, f32[624]{0:T(1024)S(1)}, bf16[768]{0:T(1024)(128)(2,1)S(1)}, f32[624,768]{1,0:T(8,128)}) fusion(bf16[624,768]{1,0:T(8,128)(2,1)S(1)} %copy-done.8, f32[624]{0:T(1024)S(1)} %copy-done.57, f32[624]{0:T(1024)S(1)} %broadcast_multiply_fusion.10, f32[768]{0:T(1024)S(1)} %copy-done.52, ...), kind=kOutput, calls=%fused_computation.82 | convolution fusion | flops 2954941952 | bytes 19111680 | tf_op jit(solution)/shard_map/dot_general | solution.py:22
  425.9 3.1 fusion.104
  430.3 2.5 convolution_convert_fusion.8.grad_ref
  432.8 14.2 %shard_map.223 = bf16[624,2304]{1,0:T(8,128)(2,1)S(1)} custom-call(bf16[624,2304]{1,0:T(8,128)(2,1)S(1)} %copy-done.1, bf16[624,768]{1,0:T(8,128)(2,1)S(1)} %convolution_convert_fusion.8.grad_ref), custom_call_target="tpu_custom_call" | custom-call | flops 996802560 | bytes 6709248 | tf_op jit(solution)/shard_map/pallas_call | solution.py:66
  447.6 7.8 fusion.97
  458.2 4.8 convolution_convert_fusion.5
  468.6 2.0 constant_dynamic-update-slice_fusion.5
  474.7 7.7 convolution_convert_fusion.3
  482.5 2.7 constant_dynamic-update-slice_fusion.3
  487.0 4.4 convolution_convert_fusion.2
  491.4 2.5 constant_dynamic-update-slice_fusion.2
  494.8 65.7 %reduce-scatter.3.cloned.1.call-done = bf16[304,768]{1,0:T(8,128)(2,1)} async-done(((bf16[9728,768]{1,0:T(8,128)(2,1)}), bf16[304,768]{1,0:T(8,128)(2,1)}) %reduce-scatter.3.cloned.1.call-update) | async-done | bytes 466960 | tf_op jit(solution)/shard_map/reduce_scatter | solution.py:282
  560.6 172.3 %reduce-scatter.5.cloned.1.call-done = bf16[304,768]{1,0:T(8,128)(2,1)} async-done(((bf16[9728,768]{1,0:T(8,128)(2,1)}), bf16[304,768]{1,0:T(8,128)(2,1)}) %reduce-scatter.5.cloned.1.call-update) | async-done | bytes 466960 | tf_op jit(solution)/shard_map/reduce_scatter | solution.py:282
  732.9 2.0 pad_maximum_fusion
  735.0 6.6 fusion.61
  744.3 3.6 copy.79
  747.9 4.3 all-to-all-start.1
  752.2 3.1 add_convert_fusion.3
  755.4 3.1 reshape.532
  758.9 2.1 copy.81
  761.0 18.9 %all-to-all-done.1 = bf16[4,3,197,192]{2,3,1,0:T(8,128)(2,1)} async-done(((bf16[4,3,197,192]{2,3,1,0:T(8,128)(2,1)}), bf16[4,3,197,192]{2,3,1,0:T(8,128)(2,1)}, u32[]{:S(2)}, u32[]{:S(2)}) %all-to-all-start.1) | async-done | bytes 907808 | tf_op jit(solution)/shard_map/all_to_all | solution.py:149
  779.9 3.8 all-to-all-start.3
  783.7 2.3 slice_select_fusion
  786.0 25.7 %all-to-all-done.3 = bf16[4,3,197,192]{2,3,1,0:T(8,128)(2,1)S(1)} async-done(((bf16[4,3,197,192]{2,3,1,0:T(8,128)(2,1)}), bf16[4,3,197,192]{2,3,1,0:T(8,128)(2,1)S(1)}, u32[]{:S(2)}, u32[]{:S(2)}) %all-to-all-start.3) | async-done | bytes 907808 | tf_op jit(solution)/shard_map/all_to_all | solution.py:149
  818.3 7.3 convert_bitcast_fusion.1
  829.0 2.1 copy.93
  831.2 2.6 copy.96
  834.1 2.5 copy.95
  836.7 6.0 copy.97
  (359 shorter events, 88.5 us)
Async XLA Ops:
  7.2 130.0 %all-gather.7.cloned.1.call-start = ((), (), s32[]{:S(2)}) async-start(), calls=%async_computation.8 | async-start | bytes 15409152 | tf_op jit(solution)/shard_map/all_gather | solution.py:177
  14.8 4.8 copy-start.30
  22.8 3.0 copy-start.70
  22.8 3.3 copy-start.37
  24.7 3.2 copy-start.36
  24.7 4.1 copy-start.39
  27.7 111.5 %copy-start.35 = (bf16[10,197,192]{1,2,0:T(8,128)(2,1)S(1)}, bf16[10,197,192]{1,2,0:T(8,128)(2,1)}, u32[]{:S(2)}) copy-start(bf16[10,197,192]{1,2,0:T(8,128)(2,1)} %param.14) | copy-start | bytes 2269444
  27.8 254.1 %all-gather.9.cloned.1.call-start = ((), (), s32[]{:S(2)}) async-start(), calls=%async_computation.9 | async-start | bytes 15409152 | tf_op jit(solution)/shard_map/all_gather | solution.py:177
  139.4 4.7 copy-start.34
  140.6 42.7 %all-to-all-start.2 = ((bf16[4,3,197,192]{2,3,1,0:T(8,128)(2,1)}), bf16[4,3,197,192]{2,3,1,0:T(8,128)(2,1)S(1)}, u32[]{:S(2)}, u32[]{:S(2)}) async-start(bf16[4,3,197,192]{2,3,1,0:T(8,128)(2,1)} %bitcast.43), calls=%async_computation.2 | async-start | bytes 2359296 | tf_op jit(solution)/shard_map/all_to_all | solution.py:143
  183.3 3.8 copy-start.17
  183.3 49.1 %all-to-all-start = ((bf16[4,3,197,192]{2,3,1,0:T(8,128)(2,1)}), bf16[4,3,197,192]{2,3,1,0:T(8,128)(2,1)S(1)}, u32[]{:S(2)}, u32[]{:S(2)}) async-start(bf16[4,3,197,192]{2,3,1,0:T(8,128)(2,1)} %bitcast.1), calls=%async_computation | async-start | bytes 2359296 | tf_op jit(solution)/shard_map/all_to_all | solution.py:143
  186.9 373.6 %reduce-scatter.3.cloned.1.call-start = ((), (), s32[]{:S(2)}) async-start(), calls=%async_computation.6 | async-start | bytes 15409152 | tf_op jit(solution)/shard_map/reduce_scatter | solution.py:282
  234.9 12.0 %copy-start.4 = (bf16[3,197,768]{2,1,0:T(8,128)(2,1)}, bf16[3,197,768]{2,1,0:T(8,128)(2,1)S(1)}, u32[]{:S(2)}) copy-start(bf16[3,197,768]{2,1,0:T(8,128)(2,1)S(1)} %reshape.499) | copy-start | bytes 2723332
  237.0 19.5 %copy-start.31 = (bf16[32,24,768]{2,1,0:T(8,128)(2,1)}, bf16[32,24,768]{2,1,0:T(8,128)(2,1)S(1)}, u32[]{:S(2)}) copy-start(bf16[32,24,768]{2,1,0:T(8,128)(2,1)S(1)} %slice.287) | copy-start | bytes 3538948
  246.8 4.2 copy-start.48
  246.8 17.9 %copy-start.64 = (f32[768]{0:T(1024)}, f32[768]{0:T(1024)S(1)}, u32[]{:S(2)}) copy-start(f32[768]{0:T(1024)S(1)} %get-tuple-element.78) | copy-start | bytes 9220
  246.9 4.1 copy-start.42
  246.9 17.8 %copy-start.51 = (f32[768]{0:T(1024)}, f32[768]{0:T(1024)S(1)}, u32[]{:S(2)}) copy-start(f32[768]{0:T(1024)S(1)} %get-tuple-element.74) | copy-start | bytes 9220
  246.9 115.1 %copy-start.54 = (f32[768]{0:T(1024)}, f32[768]{0:T(1024)S(1)}, u32[]{:S(2)}) copy-start(f32[768]{0:T(1024)S(1)} %get-tuple-element.73) | copy-start | bytes 9220
  251.0 5.5 copy-start
  257.4 14.5 %copy-start.7 = (bf16[624,768]{1,0:T(8,128)(2,1)}, bf16[624,768]{1,0:T(8,128)(2,1)S(1)}, u32[]{:S(2)}) copy-start(bf16[624,768]{1,0:T(8,128)(2,1)S(1)} %fusion.70) | copy-start | bytes 2875396
  258.1 6.6 copy-start.56
  258.1 6.6 copy-start.61
  264.7 7.2 copy-start.19
  264.8 7.2 copy-start.20
  271.9 3.3 copy-start.77
  275.2 26.3 %copy-start.24 = (bf16[624,768]{1,0:T(8,128)(2,1)}, bf16[624,768]{1,0:T(8,128)(2,1)S(1)}, u32[]{:S(2)}) copy-start(bf16[624,768]{1,0:T(8,128)(2,1)S(1)} %get-tuple-element.136) | copy-start | bytes 2875396
  275.2 86.8 %copy-start.46 = (f32[624]{0:T(1024)}, f32[624]{0:T(1024)S(1)}, u32[]{:S(2)}) copy-start(f32[624]{0:T(1024)S(1)} %broadcast_multiply_fusion.9) | copy-start | bytes 7492
  275.7 86.4 %copy-start.59 = (f32[624]{0:T(1024)}, f32[624]{0:T(1024)S(1)}, u32[]{:S(2)}) copy-start(f32[624]{0:T(1024)S(1)} %add_rsqrt_fusion.1) | copy-start | bytes 7492
  293.1 15.4 %copy-start.18 = (bf16[32,96,768]{2,1,0:T(8,128)(2,1)}, bf16[32,96,768]{2,1,0:T(8,128)(2,1)S(1)}, u32[]{:S(2)}) copy-start(bf16[32,96,768]{2,1,0:T(8,128)(2,1)S(1)} %get-tuple-element.98) | copy-start | bytes 14155780
  293.1 9.9 %slice-start.6 = ((s8[4718592]{0:T(1024)(128)(4,1)}), s8[4194304]{0:T(1024)(128)(4,1)S(1)}, s32[]{:S(2)}) async-start(s8[4718592]{0:T(1024)(128)(4,1)} %bitcast.197), calls=%async_computation.17 | async-start | bytes 8388608
  293.3 9.7 %slice-start.7 = ((s8[4718592]{0:T(1024)(128)(4,1)}), s8[524288]{0:T(1024)(128)(4,1)S(1)}, s32[]{:S(2)}) async-start(s8[4718592]{0:T(1024)(128)(4,1)} %bitcast.197), calls=%async_computation.18 | async-start | bytes 1048576
  296.0 5.5 copy-start.33
  302.5 36.0 %copy-start.21 = (bf16[624,768]{1,0:T(8,128)(2,1)}, bf16[624,768]{1,0:T(8,128)(2,1)S(1)}, u32[]{:S(2)}) copy-start(bf16[624,768]{1,0:T(8,128)(2,1)S(1)} %get-tuple-element.138) | copy-start | bytes 2875396
  303.0 5.5 copy-start.23
  320.3 8.0 copy-start.76
  342.8 14.2 %copy-start.25 = (bf16[624,768]{1,0:T(8,128)(2,1)S(1)}, bf16[624,768]{1,0:T(8,128)(2,1)}, u32[]{:S(2)}) copy-start(bf16[624,768]{1,0:T(8,128)(2,1)} %copy-done.24) | copy-start | bytes 2875396
  342.8 14.2 %copy-start.29 = (bf16[3,32,24,768]{3,2,1,0:T(8,128)(2,1)S(1)}, bf16[3,32,24,768]{3,2,1,0:T(8,128)(2,1)}, u32[]{:S(2)}) copy-start(bf16[3,32,24,768]{3,2,1,0:T(8,128)(2,1)} %copy-done.28) | copy-start | bytes 10616836
  385.2 4.2 slice-start.4
  385.3 4.3 slice-start.5
  395.5 337.3 %reduce-scatter.5.cloned.1.call-start = ((), (), s32[]{:S(2)}) async-start(), calls=%async_computation.7 | async-start | bytes 15409152 | tf_op jit(solution)/shard_map/reduce_scatter | solution.py:282
  396.7 50.9 %copy-start.44 = (f32[624]{0:T(1024)}, f32[624]{0:T(1024)S(1)}, u32[]{:S(2)}) copy-start(f32[624]{0:T(1024)S(1)} %rsqrt.44) | copy-start | bytes 7492
  400.9 12.3 %copy-start.15 = (f32[624,768]{1,0:T(8,128)}, f32[624,768]{1,0:T(8,128)S(1)}, u32[]{:S(2)}) copy-start(f32[624,768]{1,0:T(8,128)S(1)} %get-tuple-element.93) | copy-start | bytes 5750788
  400.9 12.9 %copy-start.8 = (bf16[624,768]{1,0:T(8,128)(2,1)S(1)}, bf16[624,768]{1,0:T(8,128)(2,1)}, u32[]{:S(2)}) copy-start(bf16[624,768]{1,0:T(8,128)(2,1)} %copy-done.7) | copy-start | bytes 2875396
  400.9 12.9 %copy-start.52 = (f32[768]{0:T(1024)S(1)}, f32[768]{0:T(1024)}, u32[]{:S(2)}) copy-start(f32[768]{0:T(1024)} %copy-done.51) | copy-start | bytes 9220
  400.9 12.8 %copy-start.57 = (f32[624]{0:T(1024)S(1)}, f32[624]{0:T(1024)}, u32[]{:S(2)}) copy-start(f32[624]{0:T(1024)} %copy-done.56) | copy-start | bytes 7492
  447.6 10.6 %copy-start.49 = (f32[768]{0:T(1024)S(1)}, f32[768]{0:T(1024)}, u32[]{:S(2)}) copy-start(f32[768]{0:T(1024)} %copy-done.48) | copy-start | bytes 9220
  468.6 3.1 copy-start.11
  482.5 4.5 copy-start.78
  560.5 172.4 %copy-start.38 = (bf16[304,768]{1,0:T(8,128)(2,1)S(1)}, bf16[304,768]{1,0:T(8,128)(2,1)}, u32[]{:S(2)}) copy-start(bf16[304,768]{1,0:T(8,128)(2,1)} %reduce-scatter.3.cloned.1.call-done) | copy-start | bytes 1400836
  560.5 174.4 %copy-start.50 = (f32[4,192]{1,0:T(4,128)S(1)}, f32[4,192]{1,0:T(4,128)}, u32[]{:S(2)}) copy-start(f32[4,192]{1,0:T(4,128)} %get-tuple-element.84) | copy-start | bytes 9220
  560.5 174.5 %copy-start.22 = (bf16[624,768]{1,0:T(8,128)(2,1)S(1)}, bf16[624,768]{1,0:T(8,128)(2,1)}, u32[]{:S(2)}) copy-start(bf16[624,768]{1,0:T(8,128)(2,1)} %copy-done.21) | copy-start | bytes 2875396
  560.5 252.6 %all-gather.11.cloned.1.call-start = ((), (), s32[]{:S(2)}) async-start(), calls=%async_computation.10 | async-start | bytes 8404992 | tf_op jit(solution)/shard_map/all_gather | solution.py:287
  744.3 7.9 copy-start.67
  744.3 7.9 copy-start.66
  744.3 7.9 copy-start.6
  744.3 7.9 copy-start.12
  744.3 7.9 copy-start.45
  747.9 32.0 %all-to-all-start.1 = ((bf16[4,3,197,192]{2,3,1,0:T(8,128)(2,1)}), bf16[4,3,197,192]{2,3,1,0:T(8,128)(2,1)}, u32[]{:S(2)}, u32[]{:S(2)}) async-start(bf16[4,3,197,192]{2,3,1,0:T(8,128)(2,1)} %copy.79), calls=%async_computation.1 | async-start | bytes 2359296 | tf_op jit(solution)/shard_map/all_to_all | solution.py:149
  758.9 24.8 %copy-start.73 = (pred[10]{0:T(512)(128)(4,1)S(1)}, pred[10]{0:T(512)(128)(4,1)}, u32[]{:S(2)}) copy-start(pred[10]{0:T(512)(128)(4,1)} %copy-done.72) | copy-start | bytes 34
  779.9 31.8 %all-to-all-start.3 = ((bf16[4,3,197,192]{2,3,1,0:T(8,128)(2,1)}), bf16[4,3,197,192]{2,3,1,0:T(8,128)(2,1)S(1)}, u32[]{:S(2)}, u32[]{:S(2)}) async-start(bf16[4,3,197,192]{2,3,1,0:T(8,128)(2,1)} %copy.81), calls=%async_computation.3 | async-start | bytes 2359296 | tf_op jit(solution)/shard_map/all_to_all | solution.py:149
  827.6 3.6 slice-start.2
  829.0 4.9 slice-start
  (32 other events, 65.6 us)
Sparse Core Ops, SparseCore 0:
  27.9 109.2 all-gather.6
  140.7 141.2 all-gather.8
  395.6 164.8 reduce-scatter.2
  567.5 165.3 reduce-scatter.4
  735.2 49.3 all-gather.10
